TPU v7x, 32 devices: a whole 2x2x4 slice. The times are simulated.
32 devices in a mesh: dp: 16 (over z, x, core), tensor: 2 (over y).
Axes of the slice: x: 2, y: 2, z: 4, core: 2. Of those that a mesh axis runs over, the one named last changes fastest.
Arguments:
- hidden_in: bfloat16 [4096, 1024], P('dp'), may hold values from -6 to 6
- seq_lengths: int32 [64], P('dp'), may hold values from 0 to 256, as said below
- norm_in: bfloat16 [1024], P('dp'), may hold values from 0.5 to 1.5
- w_z: bfloat16 [1024, 1536], P('dp', 'tensor'), may hold values from -0.1875 to 0.1875
- w_x: bfloat16 [1024, 1536], P('dp', 'tensor'), may hold values from -0.1875 to 0.1875
- w_bc: bfloat16 [1024, 256], P('dp'), may hold values from -0.09375 to 0.09375
- w_dt: bfloat16 [1024, 24], P('dp', 'tensor'), may hold values from -0.1875 to 0.1875
- conv_x: bfloat16 [5, 1536], P(None, 'tensor'), may hold values from -3 to 3
- conv_bc: bfloat16 [5, 256], replicated, may hold values from -3 to 3
- head_params: float32 [3, 24], P(None, 'tensor'), may hold values from -6 to 3
- w_out: bfloat16 [1536, 1024], P('tensor', 'dp'), may hold values from -0.15625 to 0.15625
- w_q: bfloat16 [1024, 512], P('dp', 'tensor'), may hold values from -0.1875 to 0.1875
- key_weight: bfloat16 [1024, 128], P('dp', 'tensor'), may hold values from -0.1875 to 0.1875
- value_weight: bfloat16 [1024, 128], P('dp', 'tensor'), may hold values from -0.1875 to 0.1875
- w_o: bfloat16 [512, 1024], P('tensor', 'dp'), may hold values from -1 to 1
- norm_mlp: bfloat16 [1024], P('dp'), may hold values from 0.5 to 1.5
- w_gate: bfloat16 [1024, 2048], P('dp', 'tensor'), may hold values from -0.1875 to 0.1875
- w_up: bfloat16 [1024, 2048], P('dp', 'tensor'), may hold values from -0.1875 to 0.1875
- w_down: bfloat16 [2048, 1024], P('tensor', 'dp'), may hold values from -0.125 to 0.125
- cotangent: bfloat16 [4096, 1024], P('dp'), may hold values from -6 to 6
Outputs:
- layer_out: float32 [4096, 1024], P('dp')
- grad_in: float32 [4096, 1024], P('dp')
- grad_norm_in: float32 [1024], P('dp')
- grad_w_z: float32 [1024, 1536], P('dp', 'tensor')
- grad_w_x: float32 [1024, 1536], P('dp', 'tensor')
- grad_w_bc: float32 [1024, 256], P('dp')
- grad_w_dt: float32 [1024, 24], P('dp', 'tensor')
- grad_conv_x: float32 [5, 1536], P(None, 'tensor')
- grad_conv_bc: float32 [5, 256], replicated
- grad_head_params: float32 [3, 24], P(None, 'tensor')
- grad_w_out: float32 [1536, 1024], P('tensor', 'dp')
- grad_w_q: float32 [1024, 512], P('dp', 'tensor')
- grad_w_k: float32 [1024, 128], P('dp', 'tensor')
- grad_w_v: float32 [1024, 128], P('dp', 'tensor')
- grad_w_o: float32 [512, 1024], P('tensor', 'dp')
- grad_norm_mlp: float32 [1024], P('dp')
- grad_w_gate: float32 [1024, 2048], P('dp', 'tensor')
- grad_w_up: float32 [1024, 2048], P('dp', 'tensor')
- grad_w_down: float32 [2048, 1024], P('tensor', 'dp')
Inputs may be any that keep to these rules, and one draw needn't show every extreme that they name: `seq_lengths`: the 4 lengths of one device sum to at most 256, and to exactly 256 on some device; rows past that sum are padding.
All inputs are finite; a program needn't handle non-finite values.
Results may differ from a plain program's by a relative error of at most 0.012.
Values may be sent and summed in bfloat16 or wider, within the bound.
A program may use at most 128 MiB of HBM per device.

v0:
```python
from functools import partial

import jax
import jax.numpy as jnp
from jax import lax
from jax.sharding import PartitionSpec as P

HEAD_WIDTH = 64


EPSILON = 1e-05
ROTARY_BASE = 100000000000.0
MASKED = -1e30
EXACT_PRODUCT = lax.Precision.HIGHEST


def product(left_side, right_side):
    return jnp.dot(left_side, right_side, preferred_element_type=jnp.float32)


def rows_product(left_side, right_side):
    return lax.dot_general(
        left_side, right_side, (((0,), (0,)), ((), ())), preferred_element_type=jnp.float32
    )


def back_product(left_side, right_side):
    return lax.dot_general(
        left_side, right_side, (((1,), (1,)), ((), ())), preferred_element_type=jnp.float32
    )


def root_norm(values, scale_row):
    return (
        values * lax.rsqrt(jnp.mean(values * values, axis=-1, keepdims=True) + EPSILON) * scale_row
    )


def layout(lengths, count_of_rows):
    row_index = jnp.arange(count_of_rows, dtype=jnp.int32)
    seq_ends = jnp.cumsum(lengths)
    segment = jnp.sum((row_index[:, None] >= seq_ends[None, :]).astype(jnp.int32), axis=1)
    slot_index = jnp.arange(lengths.shape[0], dtype=jnp.int32)
    starts = jnp.sum(jnp.where(slot_index[None, :] < segment[:, None], lengths[None, :], 0), axis=1)
    live_rows = (row_index < seq_ends[-1]).astype(jnp.float32)
    return (segment, row_index - starts, live_rows)


def rotary_embedding(values, token_position, direction):
    half_width = values.shape[-1] // 2
    frequency = ROTARY_BASE ** (-jnp.arange(half_width, dtype=jnp.float32) / half_width)
    angles = token_position.astype(jnp.float32)[:, None] * frequency[None, :]
    cosine = jnp.cos(angles)[:, None, :]
    sine_part = direction * jnp.sin(angles)[:, None, :]
    first_half = values[..., :half_width]
    second_half = values[..., half_width:]
    return jnp.concatenate(
        [
            first_half * cosine - second_half * sine_part,
            second_half * cosine + first_half * sine_part,
        ],
        axis=-1,
    )


def causal_conv(values, taps_bias, segment):
    kernel_len = taps_bias.shape[0] - 1
    conv_sum = taps_bias[kernel_len][None, :] + taps_bias[kernel_len - 1][None, :] * values
    for offset in range(1, kernel_len):
        shifted = jnp.concatenate(
            [jnp.zeros((offset, values.shape[1]), values.dtype), values[:-offset]], axis=0
        )
        earlier = jnp.concatenate([jnp.full((offset,), -1, jnp.int32), segment[:-offset]], axis=0)
        same_doc = (earlier == segment).astype(values.dtype)[:, None]
        conv_sum = conv_sum + taps_bias[kernel_len - 1 - offset][None, :] * shifted * same_doc
    return jax.nn.silu(conv_sum)


def state_mix(mixer_in, bc_act, step_raw, head_params, segment):
    count_of_rows, head_count = step_raw.shape
    state_width = bc_act.shape[1] // 2
    inputs = mixer_in.reshape(count_of_rows, head_count, -1)
    decay_rate = jnp.exp(head_params[0])
    step_size = jax.nn.softplus(step_raw + head_params[1][None, :])
    log_decay = jnp.cumsum(-step_size * decay_rate[None, :], axis=0).T
    row_index = jnp.arange(count_of_rows, dtype=jnp.int32)
    visible = (segment[:, None] == segment[None, :]) & (row_index[None, :] <= row_index[:, None])
    log_gap = log_decay[:, :, None] - log_decay[:, None, :]
    decay_mat = jnp.exp(jnp.where(visible[None], log_gap, -jnp.inf))
    intersection = jnp.dot(
        bc_act[:, state_width:], bc_act[:, :state_width].T, precision=EXACT_PRODUCT
    )
    mixing = intersection[None] * decay_mat * step_size.T[:, None, :]
    result = jnp.einsum("hts,shp->thp", mixing, inputs, precision=EXACT_PRODUCT)
    result = result + head_params[2][None, :, None] * inputs
    return result.reshape(count_of_rows, -1)


def mamba_core(gate_ssm, conv_in, step_raw, conv_taps, head_params, bc_act, segment):
    mixer_in = causal_conv(conv_in, conv_taps, segment)
    return state_mix(mixer_in, bc_act, step_raw, head_params, segment) * jax.nn.silu(gate_ssm)


def attend_forward(queries, key_matrix_rows, value_matrix_rows, visible):
    count_of_rows, head_count, head_size = queries.shape
    kv_count = key_matrix_rows.shape[1]
    grouped = queries.reshape(count_of_rows, kv_count, head_count // kv_count, head_size)
    scores = jnp.einsum(
        "tkgd,skd->kgts", grouped, key_matrix_rows, preferred_element_type=jnp.float32
    )
    logits = jnp.where(visible[None, None], scores * head_size ** (-0.5), MASKED)
    largest = jnp.max(logits, axis=-1, keepdims=True)
    weights_exp = jnp.exp(logits - largest)
    totals = jnp.sum(weights_exp, axis=-1, keepdims=True)
    attention_weights = weights_exp / totals
    attended = jnp.einsum(
        "kgts,skd->tkgd",
        attention_weights.astype(jnp.bfloat16),
        value_matrix_rows,
        preferred_element_type=jnp.float32,
    )
    return (attended.reshape(count_of_rows, head_count * head_size), largest + jnp.log(totals))


def attend_backward(queries, key_matrix_rows, value_matrix_rows, visible, log_total, grad_attended):
    count_of_rows, head_count, head_size = queries.shape
    kv_count = key_matrix_rows.shape[1]
    grouped = queries.reshape(count_of_rows, kv_count, head_count // kv_count, head_size)
    grad_grouped = grad_attended.reshape(count_of_rows, kv_count, head_count // kv_count, head_size)
    scores = jnp.einsum(
        "tkgd,skd->kgts", grouped, key_matrix_rows, preferred_element_type=jnp.float32
    )
    logits = jnp.where(visible[None, None], scores * head_size ** (-0.5), MASKED)
    attention_weights = jnp.exp(logits - log_total)
    grad_weights = jnp.einsum(
        "tkgd,skd->kgts", grad_grouped, value_matrix_rows, preferred_element_type=jnp.float32
    )
    inner_sum = jnp.sum(attention_weights * grad_weights, axis=-1, keepdims=True)
    grad_scores = (attention_weights * (grad_weights - inner_sum) * head_size ** (-0.5)).astype(
        jnp.bfloat16
    )
    grad_queries = jnp.einsum(
        "kgts,skd->tkgd", grad_scores, key_matrix_rows, preferred_element_type=jnp.float32
    )
    grad_keys = jnp.einsum(
        "kgts,tkgd->skd", grad_scores, grouped, preferred_element_type=jnp.float32
    )
    grad_values = jnp.einsum(
        "kgts,tkgd->skd",
        attention_weights.astype(jnp.bfloat16),
        grad_grouped,
        preferred_element_type=jnp.float32,
    )
    return (grad_queries.reshape(count_of_rows, head_count, head_size), grad_keys, grad_values)


def body(
    hidden_in,
    seq_lengths,
    norm_in,
    w_z,
    w_x,
    w_bc,
    w_dt,
    conv_x,
    conv_bc,
    head_params,
    w_out,
    w_q,
    key_weight,
    value_weight,
    w_o,
    norm_mlp,
    w_gate,
    w_up,
    w_down,
    cotangent,
):
    (
        gain_in,
        full_z,
        full_x,
        full_bc,
        full_dt,
        full_out,
        full_q,
        full_k,
        full_v,
        full_o,
        gain_mlp,
        full_gate,
        full_up,
        full_down,
    ) = (
        lax.all_gather(norm_in, "dp", axis=0, tiled=True),
        lax.all_gather(w_z, "dp", axis=0, tiled=True),
        lax.all_gather(w_x, "dp", axis=0, tiled=True),
        lax.all_gather(w_bc, "dp", axis=0, tiled=True),
        lax.all_gather(w_dt, "dp", axis=0, tiled=True),
        lax.all_gather(w_out, "dp", axis=1, tiled=True),
        lax.all_gather(w_q, "dp", axis=0, tiled=True),
        lax.all_gather(key_weight, "dp", axis=0, tiled=True),
        lax.all_gather(value_weight, "dp", axis=0, tiled=True),
        lax.all_gather(w_o, "dp", axis=1, tiled=True),
        lax.all_gather(norm_mlp, "dp", axis=0, tiled=True),
        lax.all_gather(w_gate, "dp", axis=0, tiled=True),
        lax.all_gather(w_up, "dp", axis=0, tiled=True),
        lax.all_gather(w_down, "dp", axis=1, tiled=True),
    )
    inputs = hidden_in.astype(jnp.float32)
    count_of_rows = inputs.shape[0]
    segment, token_position, live_rows = layout(seq_lengths, count_of_rows)
    live_column = live_rows[:, None]
    row_index = jnp.arange(count_of_rows, dtype=jnp.int32)
    visible = (segment[:, None] == segment[None, :]) & (row_index[None, :] <= row_index[:, None])
    normed_full, norm_in_pull = jax.vjp(root_norm, inputs, gain_in.astype(jnp.float32))
    normalized_input = normed_full.astype(jnp.bfloat16)
    gate_ssm = product(normalized_input, full_z)
    conv_in = product(normalized_input, full_x)
    bc_raw = product(normalized_input, full_bc)
    step_raw = product(normalized_input, full_dt)
    bc_act, bc_pull = jax.vjp(
        partial(causal_conv, segment=segment), bc_raw, conv_bc.astype(jnp.float32)
    )
    gated_full, mamba_pull = jax.vjp(
        partial(mamba_core, segment=segment),
        gate_ssm,
        conv_in,
        step_raw,
        conv_x.astype(jnp.float32),
        head_params,
        bc_act,
    )
    gated_out = gated_full.astype(jnp.bfloat16)
    query_heads = full_q.shape[1] // HEAD_WIDTH
    kv_heads = full_k.shape[1] // HEAD_WIDTH
    queries = rotary_embedding(
        product(normalized_input, full_q).reshape(count_of_rows, query_heads, HEAD_WIDTH),
        token_position,
        1.0,
    ).astype(jnp.bfloat16)
    key_matrix_rows = rotary_embedding(
        product(normalized_input, full_k).reshape(count_of_rows, kv_heads, HEAD_WIDTH),
        token_position,
        1.0,
    ).astype(jnp.bfloat16)
    value_matrix_rows = (
        product(normalized_input, full_v)
        .astype(jnp.bfloat16)
        .reshape(count_of_rows, kv_heads, HEAD_WIDTH)
    )
    attended_full, log_total = attend_forward(queries, key_matrix_rows, value_matrix_rows, visible)
    attended = attended_full.astype(jnp.bfloat16)
    local_sum = product(gated_out, full_out) + product(attended, full_o)
    mixed_sum = lax.psum(local_sum, "tensor")
    residual = inputs + live_column * mixed_sum
    normed_mlp_full, norm_mlp_pull = jax.vjp(root_norm, residual, gain_mlp.astype(jnp.float32))
    normed_mlp = normed_mlp_full.astype(jnp.bfloat16)
    gate_pre = product(normed_mlp, full_gate)
    up_pre = product(normed_mlp, full_up)
    activated = (jax.nn.silu(gate_pre) * up_pre).astype(jnp.bfloat16)
    mlp_out = lax.psum(product(activated, full_down).astype(jnp.bfloat16), "tensor").astype(
        jnp.float32
    )
    layer_out = residual + live_column * mlp_out
    (
        gain_in,
        full_z,
        full_x,
        full_bc,
        full_dt,
        full_out,
        full_q,
        full_k,
        full_v,
        full_o,
        gain_mlp,
        full_gate,
        full_up,
        full_down,
    ) = (
        lax.all_gather(norm_in, "dp", axis=0, tiled=True),
        lax.all_gather(w_z, "dp", axis=0, tiled=True),
        lax.all_gather(w_x, "dp", axis=0, tiled=True),
        lax.all_gather(w_bc, "dp", axis=0, tiled=True),
        lax.all_gather(w_dt, "dp", axis=0, tiled=True),
        lax.all_gather(w_out, "dp", axis=1, tiled=True),
        lax.all_gather(w_q, "dp", axis=0, tiled=True),
        lax.all_gather(key_weight, "dp", axis=0, tiled=True),
        lax.all_gather(value_weight, "dp", axis=0, tiled=True),
        lax.all_gather(w_o, "dp", axis=1, tiled=True),
        lax.all_gather(norm_mlp, "dp", axis=0, tiled=True),
        lax.all_gather(w_gate, "dp", axis=0, tiled=True),
        lax.all_gather(w_up, "dp", axis=0, tiled=True),
        lax.all_gather(w_down, "dp", axis=1, tiled=True),
    )
    grad_out = cotangent.astype(jnp.float32)
    grad_mlp = (live_column * grad_out).astype(jnp.bfloat16)
    grad_act = back_product(grad_mlp, full_down)
    sigmoid_gate = jax.nn.sigmoid(gate_pre)
    grad_gate = (grad_act * up_pre * sigmoid_gate * (1.0 + gate_pre * (1.0 - sigmoid_gate))).astype(
        jnp.bfloat16
    )
    grad_up = (grad_act * jax.nn.silu(gate_pre)).astype(jnp.bfloat16)
    part_down = rows_product(activated, grad_mlp)
    part_gate = rows_product(normed_mlp, grad_gate)
    part_up = rows_product(normed_mlp, grad_up)
    mlp_norm_part = back_product(grad_gate, full_gate) + back_product(grad_up, full_up)
    grad_normed_mlp = lax.psum(mlp_norm_part, "tensor")
    grad_residual_norm, part_gain_mlp = norm_mlp_pull(grad_normed_mlp)
    grad_residual = grad_out + grad_residual_norm
    grad_mixed = (live_column * grad_residual).astype(jnp.bfloat16)
    grad_gated = back_product(grad_mixed, full_out)
    grad_attended = back_product(grad_mixed, full_o).astype(jnp.bfloat16)
    part_out = rows_product(gated_out, grad_mixed)
    part_o = rows_product(attended, grad_mixed)
    grad_queries, grad_keys, grad_values = attend_backward(
        queries, key_matrix_rows, value_matrix_rows, visible, log_total, grad_attended
    )
    grad_q = (
        rotary_embedding(grad_queries, token_position, -1.0)
        .reshape(count_of_rows, -1)
        .astype(jnp.bfloat16)
    )
    grad_k = (
        rotary_embedding(grad_keys, token_position, -1.0)
        .reshape(count_of_rows, -1)
        .astype(jnp.bfloat16)
    )
    grad_v = grad_values.reshape(count_of_rows, -1).astype(jnp.bfloat16)
    grad_gate_ssm, grad_conv_in, grad_step, part_conv_x, part_heads, bc_share = mamba_pull(
        grad_gated
    )
    grad_bc_act = lax.psum(bc_share, "tensor")
    grad_bc_raw, part_conv_bc = bc_pull(grad_bc_act)
    grad_gate_ssm = grad_gate_ssm.astype(jnp.bfloat16)
    grad_conv_in = grad_conv_in.astype(jnp.bfloat16)
    grad_step = grad_step.astype(jnp.bfloat16)
    grad_bc_raw = grad_bc_raw.astype(jnp.bfloat16)
    part_z = rows_product(normalized_input, grad_gate_ssm)
    part_x = rows_product(normalized_input, grad_conv_in)
    part_bc = rows_product(normalized_input, grad_bc_raw)
    part_dt = rows_product(normalized_input, grad_step)
    part_q = rows_product(normalized_input, grad_q)
    part_k = rows_product(normalized_input, grad_k)
    part_v = rows_product(normalized_input, grad_v)
    share_weight = 1.0 / lax.axis_size("tensor")
    norm_part = (
        back_product(grad_gate_ssm, full_z)
        + back_product(grad_conv_in, full_x)
        + back_product(grad_step, full_dt)
    )
    norm_part = norm_part + back_product(grad_bc_raw, full_bc) * share_weight
    norm_part = (
        norm_part
        + back_product(grad_q, full_q)
        + back_product(grad_k, full_k)
        + back_product(grad_v, full_v)
    )
    grad_normed = lax.psum(norm_part.astype(jnp.bfloat16), "tensor").astype(jnp.float32)
    grad_input_norm, part_gain_in = norm_in_pull(grad_normed)
    grad_in = grad_residual + grad_input_norm
    sum_conv_x, sum_conv_bc, sum_heads = lax.psum((part_conv_x, part_conv_bc, part_heads), "dp")
    (
        sum_gain_in,
        sum_z,
        sum_x,
        sum_bc,
        sum_dt,
        sum_out,
        sum_q,
        sum_k,
        sum_v,
        sum_o,
        sum_gain_mlp,
        sum_gate,
        sum_up,
        sum_down,
    ) = (
        lax.psum_scatter(part_gain_in, "dp", scatter_dimension=0, tiled=True),
        lax.psum_scatter(part_z, "dp", scatter_dimension=0, tiled=True),
        lax.psum_scatter(part_x, "dp", scatter_dimension=0, tiled=True),
        lax.psum_scatter(part_bc, "dp", scatter_dimension=0, tiled=True),
        lax.psum_scatter(part_dt, "dp", scatter_dimension=0, tiled=True),
        lax.psum_scatter(part_out, "dp", scatter_dimension=1, tiled=True),
        lax.psum_scatter(part_q, "dp", scatter_dimension=0, tiled=True),
        lax.psum_scatter(part_k, "dp", scatter_dimension=0, tiled=True),
        lax.psum_scatter(part_v, "dp", scatter_dimension=0, tiled=True),
        lax.psum_scatter(part_o, "dp", scatter_dimension=1, tiled=True),
        lax.psum_scatter(part_gain_mlp, "dp", scatter_dimension=0, tiled=True),
        lax.psum_scatter(part_gate, "dp", scatter_dimension=0, tiled=True),
        lax.psum_scatter(part_up, "dp", scatter_dimension=0, tiled=True),
        lax.psum_scatter(part_down, "dp", scatter_dimension=1, tiled=True),
    )
    return (
        layer_out,
        grad_in,
        sum_gain_in,
        sum_z,
        sum_x,
        sum_bc,
        sum_dt,
        sum_conv_x,
        sum_conv_bc,
        sum_heads,
        sum_out,
        sum_q,
        sum_k,
        sum_v,
        sum_o,
        sum_gain_mlp,
        sum_gate,
        sum_up,
        sum_down,
    )


def solution(mesh):
    return jax.shard_map(
        body,
        mesh=mesh,
        in_specs=(
            P("dp", None),
            P("dp"),
            P("dp"),
            P("dp", "tensor"),
            P("dp", "tensor"),
            P("dp", None),
            P("dp", "tensor"),
            P(None, "tensor"),
            P(),
            P(None, "tensor"),
            P("tensor", "dp"),
            P("dp", "tensor"),
            P("dp", "tensor"),
            P("dp", "tensor"),
            P("tensor", "dp"),
            P("dp"),
            P("dp", "tensor"),
            P("dp", "tensor"),
            P("tensor", "dp"),
            P("dp", None),
        ),
        out_specs=(
            P("dp", None),
            P("dp", None),
            P("dp"),
            P("dp", "tensor"),
            P("dp", "tensor"),
            P("dp", None),
            P("dp", "tensor"),
            P(None, "tensor"),
            P(),
            P(None, "tensor"),
            P("tensor", "dp"),
            P("dp", "tensor"),
            P("dp", "tensor"),
            P("dp", "tensor"),
            P("tensor", "dp"),
            P("dp"),
            P("dp", "tensor"),
            P("dp", "tensor"),
            P("tensor", "dp"),
        ),
        check_vma=False,
    )
```

profile of v0, /device:TPU:9, one launch (start us, length us, event | category | flops | bytes accessed | tf_op | source)
XLA Modules:
  0.0 1318.5 jit_solution(2507230431437486949)
XLA Ops:
  17.6 23.2 %all-reduce.34 = (bf16[1024]{0:T(1024)(128)(2,1)S(1)}, bf16[1024]{0:T(1024)(128)(2,1)}) all-reduce(bf16[1024]{0:T(1024)(128)(2,1)S(1)} %dynamic-update-slice, bf16[1024]{0:T(1024)(128)(2,1)S(1)} %dynamic-update-slice.1), channel_id=1, replica_groups=mesh['dp'=16,'tensor'=2] {'dp'}, use_global_device_ids=true, to_apply=%add.29 | all-reduce | flops 2048 | bytes 8192
  41.5 26.3 %all-gather = bf16[16,64,12]{1,2,0:T(8,128)(2,1)S(1)} all-gather(bf16[1,64,12]{1,2,0:T(8,128)(2,1)} %bitcast.273), channel_id=1, replica_groups=mesh['dp'=16,'tensor'=2] {'dp'}, dimensions={0}, use_global_device_ids=true | all-gather | bytes 26112 | tf_op jit(solution)/shard_map/all_gather | solution.py:199
  68.0 2.0 negate_multiply_fusion
  70.9 20.5 %all_gather.61 = bf16[1024,64]{1,0:T(8,128)(2,1)S(1)} all-gather(bf16[64,64]{1,0:T(8,128)(2,1)} %param.32), channel_id=1, replica_groups=mesh['dp'=16,'tensor'=2] {'dp'}, dimensions={0}, use_global_device_ids=true | all-gather | bytes 139264 | tf_op jit(solution)/shard_map/all_gather | solution.py:202
  91.3 1.5 convolution_bitcast_fusion.4
  93.9 18.4 %all_gather.60 = bf16[1024,64]{1,0:T(8,128)(2,1)S(1)} all-gather(bf16[64,64]{1,0:T(8,128)(2,1)S(1)} %copy-done.96), channel_id=1, replica_groups=mesh['dp'=16,'tensor'=2] {'dp'}, dimensions={0}, use_global_device_ids=true | all-gather | bytes 139264 | tf_op jit(solution)/shard_map/all_gather | solution.py:203
  113.0 20.9 %all_gather.62 = bf16[1024,256]{1,0:T(8,128)(2,1)S(1)} all-gather(bf16[64,256]{1,0:T(8,128)(2,1)S(1)} %copy-done.71), channel_id=1, replica_groups=mesh['dp'=16,'tensor'=2] {'dp'}, dimensions={0}, use_global_device_ids=true | all-gather | bytes 557056 | tf_op jit(solution)/shard_map/all_gather | solution.py:201
  137.9 19.1 %all_gather.56 = bf16[1024,256]{1,0:T(8,128)(2,1)S(1)} all-gather(bf16[64,256]{1,0:T(8,128)(2,1)S(1)} %copy-done.72), channel_id=1, replica_groups=mesh['dp'=16,'tensor'=2] {'dp'}, dimensions={0}, use_global_device_ids=true | all-gather | bytes 557056 | tf_op jit(solution)/shard_map/all_gather | solution.py:198
  159.4 20.3 %all_gather.63 = bf16[256,1024]{0,1:T(8,128)(2,1)S(1)} all-gather(bf16[256,64]{0,1:T(8,128)(2,1)S(1)} %copy-done.73), channel_id=1, replica_groups=mesh['dp'=16,'tensor'=2] {'dp'}, dimensions={1}, use_global_device_ids=true | all-gather | bytes 557056 | tf_op jit(solution)/shard_map/all_gather | solution.py:204
  180.1 2.1 fusion.145
  182.2 2.2 fusion.58
  185.6 5.0 fusion.33
  191.8 3.1 multiply_convert_fusion.6
  195.0 2.2 fusion.155
  202.1 36.0 %all-reduce.41.cloned.1.call-done = f32[256,1024]{1,0:T(8,128)} async-done(((f32[256,1024]{1,0:T(8,128)}), f32[256,1024]{1,0:T(8,128)}) %all-reduce.41.cloned.1.call-update) | async-done | bytes 1048592 | tf_op jit(solution)/shard_map/psum | solution.py:255
  238.1 1.5 multiply_reduce_fusion.5
  239.8 41.4 %all-gather.16.cloned.1.call-done = bf16[1024,1024]{1,0:T(8,128)(2,1)} async-done(((bf16[64,1024]{1,0:T(8,128)(2,1)}), bf16[1024,1024]{1,0:T(8,128)(2,1)}) %all-gather.16.cloned.1.call-update) | async-done | bytes 2097168 | tf_op jit(solution)/shard_map/all_gather | solution.py:207
  281.2 3.3 fusion.157
  284.5 39.2 %all-gather.14.cloned.1.call-done = bf16[1024,1024]{1,0:T(8,128)(2,1)} async-done(((bf16[64,1024]{1,0:T(8,128)(2,1)}), bf16[1024,1024]{1,0:T(8,128)(2,1)}) %all-gather.14.cloned.1.call-update) | async-done | bytes 2097168 | tf_op jit(solution)/shard_map/all_gather | solution.py:206
  323.7 3.3 fusion.156
  326.9 39.3 %all-gather.18.cloned.1.call-done = bf16[1024,1024]{0,1:T(8,128)(2,1)} async-done(((bf16[1024,64]{0,1:T(8,128)(2,1)}), bf16[1024,1024]{0,1:T(8,128)(2,1)}) %all-gather.18.cloned.1.call-update) | async-done | bytes 2097168 | tf_op jit(solution)/shard_map/all_gather | solution.py:208
  366.3 4.3 multiply_convert_fusion.2
  372.6 1.7 convolution_add_fusion.4
  374.4 3.3 convolution_convert_fusion
  377.8 36.1 %all-reduce.43.cloned.1.call-done = f32[256,1024]{1,0:T(8,128)} async-done(((f32[256,1024]{1,0:T(8,128)}), f32[256,1024]{1,0:T(8,128)}) %all-reduce.43.cloned.1.call-update) | async-done | bytes 1048592 | tf_op jit(solution)/shard_map/psum | solution.py:309
  413.9 2.2 multiply_reduce_fusion.2
  416.7 1.7 multiply_convert_fusion.1
  418.8 2.5 multiply_reduce_fusion.6
  421.4 2.3 copy.93
  423.7 7.0 fusion.7
  435.8 5.1 fusion.30
  440.9 2.5 copy.94
  443.4 2.5 reduce-window.21
  446.2 3.5 multiply_reduce_fusion.10
  450.5 1.5 fusion.148
  454.5 2.1 multiply_reduce_fusion.9
  463.1 2.3 fusion.98
  465.4 7.9 all-reduce.45.cloned.1.call-done
  473.3 1.8 multiply_reduce_fusion.14
  475.8 1.5 multiply_reduce_fusion.13
  486.0 1.5 fusion.127
  489.1 2.2 fusion.161
  491.5 2.4 fusion.132
  494.0 2.4 fusion.134
  496.5 2.8 fusion.68
  500.3 2.8 fusion.164
  504.1 2.8 fusion.163
  508.9 22.5 %reduce-scatter.37.cloned.1.call-done = f32[64,12]{1,0:T(8,128)} async-done(((f32[1024,12]{1,0:T(8,128)}), f32[64,12]{1,0:T(8,128)}) %reduce-scatter.37.cloned.1.call-update) | async-done | bytes 3088
  531.4 1.4 copy.106
  532.9 42.7 %all-reduce.47.cloned.1.call-done = (bf16[256,1024]{1,0:T(8,128)(2,1)}, bf16[256,1024]{1,0:T(8,128)(2,1)}) async-done(((bf16[256,1024]{1,0:T(8,128)(2,1)}, bf16[256,1024]{1,0:T(8,128)(2,1)}), (bf16[256,1024]{1,0:T(8,128)(2,1)}, bf16[256,1024]{1,0:T(8,128)(2,1)})) %all-reduce.47.cloned.1.call-update) | async-done | bytes 1048592 | tf_op jit(solution)/shard_map/psum | solution.py:262
  575.6 1.5 fusion.45
  577.1 49.1 %all-reduce.33 = (f32[1024]{0:T(1024)S(1)}, f32[5,768]{1,0:T(8,128)}, f32[5,256]{1,0:T(8,128)}, f32[3,12]{1,0:T(4,128)}, f32[1024]{0:T(1024)S(1)}) all-reduce(f32[1024]{0:T(1024)S(1)} %get-tuple-element.25, f32[5,768]{1,0:T(8,128)S(1)} %pad_add_fusion.1, ...), channel_id=2, replica_groups=mesh['dp'=16,'tensor'=2] {'dp'}, use_global_device_ids=true, to_apply=%region_24.25.clone | all-reduce | flops 7204 | bytes 57632
  627.4 3.2 fusion.46
  630.6 3.0 reduce-scatter.27.cloned.1.call-done
  633.6 59.1 %reduce-scatter.25.cloned.1.call-done = f32[64,64]{1,0:T(8,128)} async-done(((f32[1024,64]{1,0:T(8,128)}), f32[64,64]{1,0:T(8,128)}) %reduce-scatter.25.cloned.1.call-update) | async-done | bytes 16400 | tf_op jit(solution)/shard_map/reduce_scatter | solution.py:387
  692.7 60.9 %reduce-scatter.29.cloned.1.call-done = f32[256,64]{0,1:T(8,128)} async-done(((f32[256,1024]{0,1:T(8,128)}), f32[256,64]{0,1:T(8,128)}) %reduce-scatter.29.cloned.1.call-update) | async-done | bytes 65552 | tf_op jit(solution)/shard_map/reduce_scatter | solution.py:389
  753.6 60.5 %reduce-scatter.23.cloned.1.call-done = f32[64,256]{1,0:T(8,128)} async-done(((f32[1024,256]{1,0:T(8,128)}), f32[64,256]{1,0:T(8,128)}) %reduce-scatter.23.cloned.1.call-update) | async-done | bytes 65552 | tf_op jit(solution)/shard_map/reduce_scatter | solution.py:386
  814.1 60.9 %reduce-scatter.19.cloned.1.call-done = f32[64,256]{1,0:T(8,128)} async-done(((f32[1024,256]{1,0:T(8,128)}), f32[64,256]{1,0:T(8,128)}) %reduce-scatter.19.cloned.1.call-update) | async-done | bytes 65552 | tf_op jit(solution)/shard_map/reduce_scatter | solution.py:383
  875.1 69.8 %reduce-scatter.21.cloned.1.call-done = f32[768,64]{0,1:T(8,128)} async-done(((f32[768,1024]{0,1:T(8,128)}), f32[768,64]{0,1:T(8,128)}) %reduce-scatter.21.cloned.1.call-update) | async-done | bytes 196624 | tf_op jit(solution)/shard_map/reduce_scatter | solution.py:385
  944.8 69.5 %reduce-scatter.17.cloned.1.call-done = f32[64,768]{1,0:T(8,128)} async-done(((f32[1024,768]{1,0:T(8,128)}), f32[64,768]{1,0:T(8,128)}) %reduce-scatter.17.cloned.1.call-update) | async-done | bytes 196624 | tf_op jit(solution)/shard_map/reduce_scatter | solution.py:382
  1014.4 69.5 %reduce-scatter.15.cloned.1.call-done = f32[64,768]{1,0:T(8,128)} async-done(((f32[1024,768]{1,0:T(8,128)}), f32[64,768]{1,0:T(8,128)}) %reduce-scatter.15.cloned.1.call-update) | async-done | bytes 196624 | tf_op jit(solution)/shard_map/reduce_scatter | solution.py:381
  1083.9 75.3 %reduce-scatter.35.cloned.1.call-done = f32[1024,64]{0,1:T(8,128)} async-done(((f32[1024,1024]{0,1:T(8,128)}), f32[1024,64]{0,1:T(8,128)}) %reduce-scatter.35.cloned.1.call-update) | async-done | bytes 262160 | tf_op jit(solution)/shard_map/reduce_scatter | solution.py:393
  1159.2 76.4 %reduce-scatter.33.cloned.1.call-done = f32[64,1024]{1,0:T(8,128)} async-done(((f32[1024,1024]{1,0:T(8,128)}), f32[64,1024]{1,0:T(8,128)}) %reduce-scatter.33.cloned.1.call-update) | async-done | bytes 262160 | tf_op jit(solution)/shard_map/reduce_scatter | solution.py:392
  1235.6 75.9 %reduce-scatter.31.cloned.1.call-done = f32[64,1024]{1,0:T(8,128)} async-done(((f32[1024,1024]{1,0:T(8,128)}), f32[64,1024]{1,0:T(8,128)}) %reduce-scatter.31.cloned.1.call-update) | async-done | bytes 262160 | tf_op jit(solution)/shard_map/reduce_scatter | solution.py:391
  (404 shorter events, 59.9 us)
Async XLA Ops:
  7.2 105.1 %copy-start = (bf16[256,1024]{1,0:T(8,128)(2,1)S(1)}, bf16[256,1024]{1,0:T(8,128)(2,1)}, u32[]{:S(2)}) copy-start(bf16[256,1024]{1,0:T(8,128)(2,1)} %param.20) | copy-start | bytes 1572868
  7.2 86.7 %copy-start.96 = (bf16[64,64]{1,0:T(8,128)(2,1)S(1)}, bf16[64,64]{1,0:T(8,128)(2,1)}, u32[]{:S(2)}) copy-start(bf16[64,64]{1,0:T(8,128)(2,1)} %param.33) | copy-start | bytes 24580
  7.2 105.8 %copy-start.71 = (bf16[64,256]{1,0:T(8,128)(2,1)S(1)}, bf16[64,256]{1,0:T(8,128)(2,1)}, u32[]{:S(2)}) copy-start(bf16[64,256]{1,0:T(8,128)(2,1)} %param.31) | copy-start | bytes 98308
  7.2 172.9 %all-gather.8.cloned.1.call-start = ((), (), s32[]{:S(2)}) async-start(), calls=%async_computation.12 | async-start | bytes 1671168 | tf_op jit(solution)/shard_map/all_gather | solution.py:197
  8.0 183.9 %all-gather.10.cloned.1.call-start = ((), (), s32[]{:S(2)}) async-start(), calls=%async_computation.13 | async-start | bytes 1671168 | tf_op jit(solution)/shard_map/all_gather | solution.py:196
  8.7 186.2 %all-gather.12.cloned.1.call-start = ((), (), s32[]{:S(2)}) async-start(), calls=%async_computation.14 | async-start | bytes 1671168 | tf_op jit(solution)/shard_map/all_gather | solution.py:200
  9.4 228.7 %all-reduce.41.cloned.1.call-start = ((), (), s32[]{:S(2)}) async-start(), calls=%async_computation.15 | async-start | bytes 2097152 | tf_op jit(solution)/shard_map/psum | solution.py:255
  9.5 124.9 %copy-start.107 = (f32[32]{0:T(128)}, f32[32]{0:T(128)S(1)}, u32[]{:S(2)}) copy-start(f32[32]{0:T(128)S(1)} %multiply_power_fusion) | copy-start | bytes 388
  10.4 31.2 %copy-start.121 = (s32[4,1]{0,1:T(1,128)}, s32[4,1]{0,1:T(1,128)S(1)}, u32[]{:S(2)}) copy-start(s32[4,1]{0,1:T(1,128)S(1)} %reduce-window.16) | copy-start | bytes 52
  12.5 80.3 %copy-start.104 = (f32[256]{0:T(256)}, f32[256]{0:T(256)S(1)}, u32[]{:S(2)}) copy-start(f32[256]{0:T(256)S(1)} %fusion.47) | copy-start | bytes 3076
  12.5 121.9 %copy-start.84 = (f32[256]{0:T(256)}, f32[256]{0:T(256)S(1)}, u32[]{:S(2)}) copy-start(f32[256]{0:T(256)S(1)} %subtract_convert_fusion.2) | copy-start | bytes 3076
  13.9 78.9 %copy-start.116 = (f32[12]{0:T(128)}, f32[12]{0:T(128)S(1)}, u32[]{:S(2)}) copy-start(f32[12]{0:T(128)S(1)} %get-tuple-element.99) | copy-start | bytes 148
  67.9 66.5 %copy-start.55 = (bf16[1024,12]{0,1:T(8,128)(2,1)}, bf16[1024,12]{0,1:T(8,128)(2,1)S(1)}, u32[]{:S(2)}) copy-start(bf16[1024,12]{0,1:T(8,128)(2,1)S(1)} %reshape.618) | copy-start | bytes 73732
  91.3 20.9 %copy-start.35 = (bf16[1024,64]{1,0:T(8,128)(2,1)}, bf16[1024,64]{1,0:T(8,128)(2,1)S(1)}, u32[]{:S(2)}) copy-start(bf16[1024,64]{1,0:T(8,128)(2,1)S(1)} %all_gather.61) | copy-start | bytes 393220
  93.7 41.9 %copy-start.43 = (f32[256,32]{0,1:T(8,128)}, f32[256,32]{0,1:T(8,128)S(1)}, u32[]{:S(2)}) copy-start(f32[256,32]{0,1:T(8,128)S(1)} %get-tuple-element.102) | copy-start | bytes 98308
  93.9 43.3 %copy-start.59 = (bf16[256,32]{0,1:T(8,128)(2,1)}, bf16[256,32]{0,1:T(8,128)(2,1)S(1)}, u32[]{:S(2)}) copy-start(bf16[256,32]{0,1:T(8,128)(2,1)S(1)} %get-tuple-element.87) | copy-start | bytes 49156
  93.9 43.2 %copy-start.61 = (bf16[256,32]{0,1:T(8,128)(2,1)}, bf16[256,32]{0,1:T(8,128)(2,1)S(1)}, u32[]{:S(2)}) copy-start(bf16[256,32]{0,1:T(8,128)(2,1)S(1)} %get-tuple-element.88) | copy-start | bytes 49156
  112.3 25.5 %copy-start.106 = (bf16[5,256]{1,0:T(8,128)(2,1)S(1)}, bf16[5,256]{1,0:T(8,128)(2,1)}, u32[]{:S(2)}) copy-start(bf16[5,256]{1,0:T(8,128)(2,1)} %param.28) | copy-start | bytes 7684
  112.3 25.5 %copy-start.72 = (bf16[64,256]{1,0:T(8,128)(2,1)S(1)}, bf16[64,256]{1,0:T(8,128)(2,1)}, u32[]{:S(2)}) copy-start(bf16[64,256]{1,0:T(8,128)(2,1)} %param.25) | copy-start | bytes 98308
  113.0 66.7 %copy-start.69 = (bf16[256,64,1]{0,1,2:T(8,128)(2,1)}, bf16[256,64,1]{0,1,2:T(8,128)(2,1)S(1)}, u32[]{:S(2)}) copy-start(bf16[256,64,1]{0,1,2:T(8,128)(2,1)S(1)} %fusion.41) | copy-start | bytes 98308
  135.4 44.6 %copy-start.1 = (f32[1,4,256,256]{2,3,1,0:T(8,128)}, f32[1,4,256,256]{2,3,1,0:T(8,128)S(1)}, u32[]{:S(2)}) copy-start(f32[1,4,256,256]{2,3,1,0:T(8,128)S(1)} %get-tuple-element.112) | copy-start | bytes 3145732
  135.4 44.6 %copy-start.86 = (f32[4,256]{1,0:T(4,128)}, f32[4,256]{1,0:T(4,128)S(1)}, u32[]{:S(2)}) copy-start(f32[4,256]{1,0:T(4,128)S(1)} %get-tuple-element.111) | copy-start | bytes 12292
  135.4 23.9 %copy-start.73 = (bf16[256,64]{0,1:T(8,128)(2,1)S(1)}, bf16[256,64]{0,1:T(8,128)(2,1)}, u32[]{:S(2)}) copy-start(bf16[256,64]{0,1:T(8,128)(2,1)} %param.34) | copy-start | bytes 98308
  135.6 44.4 %copy-start.88 = (f32[4,256]{1,0:T(4,128)}, f32[4,256]{1,0:T(4,128)S(1)}, u32[]{:S(2)}) copy-start(f32[4,256]{1,0:T(4,128)S(1)} %fusion.50) | copy-start | bytes 12292
  135.7 23.6 %copy-start.76 = (f32[256]{0:T(256)}, f32[256]{0:T(256)S(1)}, u32[]{:S(2)}) copy-start(f32[256]{0:T(256)S(1)} %get-tuple-element.103) | copy-start | bytes 3076
  135.7 23.6 %copy-start.78 = (f32[256]{0:T(256)}, f32[256]{0:T(256)S(1)}, u32[]{:S(2)}) copy-start(f32[256]{0:T(256)S(1)} %get-tuple-element.105) | copy-start | bytes 3076
  135.7 23.6 %copy-start.80 = (f32[256]{0:T(256)}, f32[256]{0:T(256)S(1)}, u32[]{:S(2)}) copy-start(f32[256]{0:T(256)S(1)} %get-tuple-element.104) | copy-start | bytes 3076
  136.4 45.8 %copy-start.63 = (f32[768]{0:T(1024)}, f32[768]{0:T(1024)S(1)}, u32[]{:S(2)}) copy-start(f32[768]{0:T(1024)S(1)} %get-tuple-element.35) | copy-start | bytes 9220
  136.4 45.8 %copy-start.65 = (f32[768]{0:T(1024)}, f32[768]{0:T(1024)S(1)}, u32[]{:S(2)}) copy-start(f32[768]{0:T(1024)S(1)} %get-tuple-element.34) | copy-start | bytes 9220
  137.8 21.5 %copy-start.100 = (f32[1,256]{1,0:T(1,128)}, f32[1,256]{1,0:T(1,128)S(1)}, u32[]{:S(2)}) copy-start(f32[1,256]{1,0:T(1,128)S(1)} %get-tuple-element.93) | copy-start | bytes 3076
  137.8 21.5 %copy-start.101 = (f32[1,256]{1,0:T(1,128)}, f32[1,256]{1,0:T(1,128)S(1)}, u32[]{:S(2)}) copy-start(f32[1,256]{1,0:T(1,128)S(1)} %get-tuple-element.94) | copy-start | bytes 3076
  137.8 21.5 %copy-start.102 = (f32[1,256]{1,0:T(1,128)}, f32[1,256]{1,0:T(1,128)S(1)}, u32[]{:S(2)}) copy-start(f32[1,256]{1,0:T(1,128)S(1)} %get-tuple-element.95) | copy-start | bytes 3076
  137.8 21.5 %copy-start.103 = (f32[1,256]{1,0:T(1,128)}, f32[1,256]{1,0:T(1,128)S(1)}, u32[]{:S(2)}) copy-start(f32[1,256]{1,0:T(1,128)S(1)} %get-tuple-element.96) | copy-start | bytes 3076
  179.7 17.4 %copy-start.10 = (bf16[256,1024]{0,1:T(8,128)(2,1)}, bf16[256,1024]{0,1:T(8,128)(2,1)S(1)}, u32[]{:S(2)}) copy-start(bf16[256,1024]{0,1:T(8,128)(2,1)S(1)} %all_gather.63) | copy-start | bytes 1572868
  198.5 82.7 %all-gather.16.cloned.1.call-start = ((), (), s32[]{:S(2)}) async-start(), calls=%async_computation.17 | async-start | bytes 2228224 | tf_op jit(solution)/shard_map/all_gather | solution.py:207
  199.1 124.6 %all-gather.14.cloned.1.call-start = ((), (), s32[]{:S(2)}) async-start(), calls=%async_computation.16 | async-start | bytes 2228224 | tf_op jit(solution)/shard_map/all_gather | solution.py:206
  199.7 166.6 %all-gather.18.cloned.1.call-start = ((), (), s32[]{:S(2)}) async-start(), calls=%async_computation.18 | async-start | bytes 2228224 | tf_op jit(solution)/shard_map/all_gather | solution.py:208
  200.4 213.4 %all-reduce.43.cloned.1.call-start = ((), (), s32[]{:S(2)}) async-start(), calls=%async_computation.19 | async-start | bytes 2097152 | tf_op jit(solution)/shard_map/psum | solution.py:309
  202.1 214.0 %copy-start.82 = (f32[256]{0:T(256)}, f32[256]{0:T(256)S(1)}, u32[]{:S(2)}) copy-start(f32[256]{0:T(256)S(1)} %compare_convert_fusion.3) | copy-start | bytes 3076
  239.7 176.5 %copy-start.74 = (f32[256]{0:T(256)}, f32[256]{0:T(256)S(1)}, u32[]{:S(2)}) copy-start(f32[256]{0:T(256)S(1)} %fusion.115) | copy-start | bytes 3076
  374.3 99.0 %all-reduce.45.cloned.1.call-start = ((), (), s32[]{:S(2)}) async-start(), calls=%async_computation.20 | async-start | bytes 524288 | tf_op jit(solution)/shard_map/psum | solution.py:334
  450.4 81.0 %reduce-scatter.37.cloned.1.call-start = ((), (), s32[]{:S(2)}) async-start(), calls=%async_computation.32 | async-start | bytes 557056
  462.0 113.6 %all-reduce.47.cloned.1.call-start = ((), (), s32[]{:S(2)}) async-start(), calls=%async_computation.33 | async-start | bytes 2097152 | tf_op jit(solution)/shard_map/psum | solution.py:262
  481.9 151.7 %reduce-scatter.27.cloned.1.call-start = ((), (), s32[]{:S(2)}) async-start(), calls=%async_computation.27 | async-start | bytes 557056 | tf_op jit(solution)/shard_map/reduce_scatter | solution.py:388
  483.2 209.5 %reduce-scatter.25.cloned.1.call-start = ((), (), s32[]{:S(2)}) async-start(), calls=%async_computation.26 | async-start | bytes 557056 | tf_op jit(solution)/shard_map/reduce_scatter | solution.py:387
  484.6 269.1 %reduce-scatter.29.cloned.1.call-start = ((), (), s32[]{:S(2)}) async-start(), calls=%async_computation.28 | async-start | bytes 1114112 | tf_op jit(solution)/shard_map/reduce_scatter | solution.py:389
  486.0 328.1 %reduce-scatter.23.cloned.1.call-start = ((), (), s32[]{:S(2)}) async-start(), calls=%async_computation.25 | async-start | bytes 1114112 | tf_op jit(solution)/shard_map/reduce_scatter | solution.py:386
  487.6 387.5 %reduce-scatter.19.cloned.1.call-start = ((), (), s32[]{:S(2)}) async-start(), calls=%async_computation.23 | async-start | bytes 1114112 | tf_op jit(solution)/shard_map/reduce_scatter | solution.py:383
  489.1 455.8 %reduce-scatter.21.cloned.1.call-start = ((), (), s32[]{:S(2)}) async-start(), calls=%async_computation.24 | async-start | bytes 3342336 | tf_op jit(solution)/shard_map/reduce_scatter | solution.py:385
  491.4 522.9 %reduce-scatter.17.cloned.1.call-start = ((), (), s32[]{:S(2)}) async-start(), calls=%async_computation.22 | async-start | bytes 3342336 | tf_op jit(solution)/shard_map/reduce_scatter | solution.py:382
  493.9 590.0 %reduce-scatter.15.cloned.1.call-start = ((), (), s32[]{:S(2)}) async-start(), calls=%async_computation.21 | async-start | bytes 3342336 | tf_op jit(solution)/shard_map/reduce_scatter | solution.py:381
  496.4 662.7 %reduce-scatter.35.cloned.1.call-start = ((), (), s32[]{:S(2)}) async-start(), calls=%async_computation.31 | async-start | bytes 4456448 | tf_op jit(solution)/shard_map/reduce_scatter | solution.py:393
  499.3 736.3 %reduce-scatter.33.cloned.1.call-start = ((), (), s32[]{:S(2)}) async-start(), calls=%async_computation.30 | async-start | bytes 4456448 | tf_op jit(solution)/shard_map/reduce_scatter | solution.py:392
  503.1 808.3 %reduce-scatter.31.cloned.1.call-start = ((), (), s32[]{:S(2)}) async-start(), calls=%async_computation.29 | async-start | bytes 4456448 | tf_op jit(solution)/shard_map/reduce_scatter | solution.py:391
  507.0 25.8 %copy-start.109 = (f32[256]{0:T(256)S(1)}, f32[256]{0:T(256)}, u32[]{:S(2)}) copy-start(f32[256]{0:T(256)} %get-tuple-element.49) | copy-start | bytes 3076
  507.0 25.8 %copy-start.110 = (f32[256]{0:T(256)S(1)}, f32[256]{0:T(256)}, u32[]{:S(2)}) copy-start(f32[256]{0:T(256)} %get-tuple-element.52) | copy-start | bytes 3076
  507.0 25.8 %copy-start.111 = (f32[256]{0:T(256)S(1)}, f32[256]{0:T(256)}, u32[]{:S(2)}) copy-start(f32[256]{0:T(256)} %get-tuple-element.83) | copy-start | bytes 3076
  507.0 25.8 %copy-start.112 = (f32[256]{0:T(256)S(1)}, f32[256]{0:T(256)}, u32[]{:S(2)}) copy-start(f32[256]{0:T(256)} %get-tuple-element.29) | copy-start | bytes 3076
  507.0 25.8 %copy-start.113 = (f32[256]{0:T(256)S(1)}, f32[256]{0:T(256)}, u32[]{:S(2)}) copy-start(f32[256]{0:T(256)} %get-tuple-element.30) | copy-start | bytes 3076
  507.0 70.1 %copy-start.95 = (f32[1024]{0:T(1024)S(1)}, f32[1024]{0:T(1024)}, u32[]{:S(2)}) copy-start(f32[1024]{0:T(1024)} %get-tuple-element.23) | copy-start | bytes 12292
  507.0 120.3 %copy-start.105 = (f32[256]{0:T(256)S(1)}, f32[256]{0:T(256)}, u32[]{:S(2)}) copy-start(f32[256]{0:T(256)} %copy-done.104) | copy-start | bytes 3076
  507.1 120.3 %copy-start.3 = (f32[256,1024]{1,0:T(8,128)S(1)}, f32[256,1024]{1,0:T(8,128)}, u32[]{:S(2)}) copy-start(f32[256,1024]{1,0:T(8,128)} %all-reduce.43.cloned.1.call-done) | copy-start | bytes 3145732
  507.1 120.3 %copy-start.75 = (f32[256]{0:T(256)S(1)}, f32[256]{0:T(256)}, u32[]{:S(2)}) copy-start(f32[256]{0:T(256)} %copy-done.74) | copy-start | bytes 3076
  507.1 120.3 %copy-start.99 = (f32[256]{0:T(256)S(1)}, f32[256]{0:T(256)}, u32[]{:S(2)}) copy-start(f32[256]{0:T(256)} %copy-done.98) | copy-start | bytes 3076
  (82 other events, 277.3 us)
Sparse Core Ops, SparseCore 0:
  10.3 40.2 all-gather.7
  52.9 39.2 all-gather.9
  94.5 40.2 all-gather.11
  198.6 39.4 all-reduce.40
  240.3 40.8 all-gather.15
  283.5 40.1 all-gather.13
  326.1 40.1 all-gather.17
  374.5 39.3 all-reduce.42
  450.5 22.7 all-reduce.44
  477.1 54.2 reduce-scatter.36
  534.3 41.2 all-reduce.46
  580.0 53.5 reduce-scatter.26
  637.7 54.9 reduce-scatter.24
  697.2 56.3 reduce-scatter.28
  757.7 56.3 reduce-scatter.22
  818.6 56.4 reduce-scatter.18
  879.3 65.5 reduce-scatter.20
  949.1 65.2 reduce-scatter.16
  1018.7 65.1 reduce-scatter.14
  1088.2 70.9 reduce-scatter.34
  1164.1 71.4 reduce-scatter.32
  1240.0 71.4 reduce-scatter.30
where the time goes:
time: 1330 us; the launch traced here: 1320 us
  waiting for transfers between devices  950 us (71%)
  blocking collectives  198 us (15%)
  matrix products  86.5 us (7%)
  other arithmetic  42.3 us (3%)
  local copies, waits for them, and re-layouts  22.9 us (2%)
  between operations  17.6 us (1%)
    reduce_scatter x1, waiting for transfers between devices, body(): lax.psum_scatter(part_up, 'dp', scatter_dimension=0, tiled=True)  76.4 us
    reduce_scatter x1, waiting for transfers between devices, body(): lax.psum_scatter(part_gate, 'dp', scatter_dimension=0, tiled=True)  75.9 us
    reduce_scatter x1, waiting for transfers between devices, body(): lax.psum_scatter(part_down, 'dp', scatter_dimension=1, tiled=True)  75.3 us
    unnamed x2, blocking collectives  72.3 us
    reduce_scatter x1, waiting for transfers between devices, body(): lax.psum_scatter(part_out, 'dp', scatter_dimension=1, tiled=True)  69.8 us
    reduce_scatter x1, waiting for transfers between devices, body(): lax.psum_scatter(part_z, 'dp', scatter_dimension=0, tiled=True)  69.5 us
    reduce_scatter x1, waiting for transfers between devices, body(): lax.psum_scatter(part_x, 'dp', scatter_dimension=0, tiled=True)  69.5 us
    reduce_scatter x1, waiting for transfers between devices, body(): lax.psum_scatter(part_bc, 'dp', scatter_dimension=0, tiled=True)  60.9 us
  transfers between devices with their start and end apart: 22, of which 19 were waited for; matrix products, arithmetic and copies ran while one was open for 8% of the time, Pallas kernels for 0%

commit v1 on v0

--- a/solution.py
+++ b/solution.py
@@ -3,6 +3,8 @@
 import jax
 import jax.numpy as jnp
 from jax import lax
+from jax.experimental import pallas as pl
+from jax.experimental.pallas import tpu as pltpu
 from jax.sharding import PartitionSpec as P
 
 HEAD_WIDTH = 64
@@ -152,6 +154,346 @@
         preferred_element_type=jnp.float32,
     )
     return (grad_queries.reshape(count_of_rows, head_count, head_size), grad_keys, grad_values)
+
+
+MESH = pl.DeviceIdType.MESH
+VMEM_BYTES = 52 * 1024 * 1024
+ADD_ROWS = 16
+
+
+def place(count):
+    me = lax.axis_index("dp")
+    core = lax.rem(me, 2)
+    column = lax.rem(lax.div(me, 2), 2)
+    line = lax.div(me, 4)
+    return me, line, column, core, count // 4
+
+
+def dp_index(line, column, core):
+    return (line * 2 + column) * 2 + core
+
+
+def greet(peers):
+    barrier = pltpu.get_barrier_semaphore()
+    for peer in peers:
+        pl.semaphore_signal(barrier, inc=1, device_id={"dp": peer}, device_id_type=MESH)
+    pl.semaphore_wait(barrier, len(peers))
+
+
+def gather_kernel(count, arrays, *refs):
+    shards, wholes = refs[:arrays], refs[arrays : 2 * arrays]
+    own_sem, line_send, line_recv, side_send, side_recv, core_send, core_recv = refs[2 * arrays :]
+    me, line, column, core, length = place(count)
+    side = dp_index(line, 1 - column, core)
+    sibling = dp_index(line, column, 1 - core)
+    ahead = [dp_index(lax.rem(line + d, length), column, core) for d in range(1, length)]
+    greet(ahead + [side, sibling])
+
+    def rows(array, index):
+        size = shards[array].shape[0]
+        return wholes[array].at[pl.ds(pl.multiple_of(index * size, size), size)]
+
+    def send(source, target, send_sem, recv_sem, peer):
+        copy = pltpu.make_async_remote_copy(
+            src_ref=source,
+            dst_ref=target,
+            send_sem=send_sem,
+            recv_sem=recv_sem,
+            device_id={"dp": peer},
+            device_id_type=MESH,
+        )
+        copy.start()
+        return copy
+
+    own, line_copies, side_copies, core_copies = [], {}, {}, {}
+    for k in range(arrays):
+        mine = rows(k, me)
+        side_copies[k, 0] = send(
+            shards[k], mine, side_send.at[k, 0], side_recv.at[k, 0], side
+        )
+        for d in range(1, length):
+            line_copies[k, d] = send(
+                shards[k], mine, line_send.at[k, d], line_recv.at[k, d], ahead[d - 1]
+            )
+        core_copies[k, 0] = send(
+            shards[k], mine, core_send.at[k, 0], core_recv.at[k, 0], sibling
+        )
+        copy = pltpu.make_async_copy(shards[k], mine, own_sem.at[k])
+        copy.start()
+        own.append(copy)
+
+    def pass_side(k):
+        for d in range(length):
+            side_copies[k, d].wait_recv()
+            block = rows(k, dp_index(lax.rem(line - d + length, length), 1 - column, core))
+            j = length + d
+            core_copies[k, j] = send(
+                block, block, core_send.at[k, j], core_recv.at[k, j], sibling
+            )
+
+    for k in range(arrays):
+        for d in range(1, length):
+            line_copies[k, d].wait_recv()
+            block = rows(k, dp_index(lax.rem(line - d + length, length), column, core))
+            side_copies[k, d] = send(
+                block, block, side_send.at[k, d], side_recv.at[k, d], side
+            )
+            core_copies[k, d] = send(
+                block, block, core_send.at[k, d], core_recv.at[k, d], sibling
+            )
+        if k:
+            pass_side(k - 1)
+    pass_side(arrays - 1)
+    for copy in own:
+        copy.wait()
+    for copy in core_copies.values():
+        copy.wait()
+    for copy in list(line_copies.values()) + list(side_copies.values()):
+        copy.wait_send()
+
+
+def gather_rows(shards, count, collective_id):
+    if shards[0].shape[0] % 16 or count % 4:
+        return tuple(lax.all_gather(shard, "dp", axis=0, tiled=True) for shard in shards)
+    arrays, length = len(shards), count // 4
+    return pl.pallas_call(
+        partial(gather_kernel, count, arrays),
+        out_shape=tuple(
+            jax.ShapeDtypeStruct((count * s.shape[0], s.shape[1]), s.dtype) for s in shards
+        ),
+        in_specs=[pl.BlockSpec(memory_space=pl.ANY)] * arrays,
+        out_specs=(pl.BlockSpec(memory_space=pl.ANY),) * arrays,
+        scratch_shapes=[pltpu.SemaphoreType.DMA((arrays,))]
+        + [pltpu.SemaphoreType.DMA((arrays, length))] * 4
+        + [pltpu.SemaphoreType.DMA((arrays, 2 * length))] * 2,
+        compiler_params=pltpu.CompilerParams(collective_id=collective_id, has_side_effects=True),
+    )(*shards)
+
+
+def scatter_kernel(count, arrays, *refs):
+    parts, small = refs[:arrays], refs[arrays]
+    sums, small_sum = refs[arrays + 1 : 2 * arrays + 1], refs[2 * arrays + 1]
+    rest = refs[2 * arrays + 2 :]
+    from_core, from_side, from_line = (
+        rest[:arrays],
+        rest[arrays : 2 * arrays],
+        rest[2 * arrays : 3 * arrays],
+    )
+    small_core, small_pair, small_side, small_line = rest[3 * arrays : 3 * arrays + 4]
+    core_send, core_recv, side_send, side_recv, line_send, line_recv = rest[3 * arrays + 4 :]
+    me, line, column, core, length = place(count)
+    side = dp_index(line, 1 - column, core)
+    sibling = dp_index(line, column, 1 - core)
+    ahead = [dp_index(lax.rem(line + d, length), column, core) for d in range(1, length)]
+    greet(ahead + [side, sibling])
+
+    def send(source, target, send_sem, recv_sem, peer):
+        copy = pltpu.make_async_remote_copy(
+            src_ref=source,
+            dst_ref=target,
+            send_sem=send_sem,
+            recv_sem=recv_sem,
+            device_id={"dp": peer},
+            device_id_type=MESH,
+        )
+        copy.start()
+        return copy
+
+    def part_start(k, d, block_column, block_core):
+        size = sums[k].shape[0]
+        return pl.multiple_of(
+            dp_index(lax.rem(line + d, length), block_column, block_core) * size, size
+        )
+
+    def add_into(target, terms, size):
+        @pl.loop(0, size // ADD_ROWS)
+        def _(step):
+            shift = step * ADD_ROWS
+            total = None
+            for ref, start in terms:
+                at = pl.ds(pl.multiple_of(start + shift, ADD_ROWS), ADD_ROWS)
+                value = ref[at, :].astype(jnp.float32)
+                total = value if total is None else total + value
+            ref, start = target
+            at = pl.ds(pl.multiple_of(start + shift, ADD_ROWS), ADD_ROWS)
+            ref[at, :] = total.astype(ref.dtype)
+
+    core_copies, side_copies, line_copies = {}, {}, {}
+    last = arrays
+    order = list(range(1, length)) + [0]
+    core_copies[last, 0] = send(
+        small, small_core, core_send.at[last, 0], core_recv.at[last, 0], sibling
+    )
+    for other in (1, 0):
+        for k in range(arrays):
+            size = sums[k].shape[0]
+            for d in order:
+                j = other * length + d
+                block_column = 1 - column if other else column
+                start = part_start(k, d, block_column, 1 - core)
+                core_copies[k, j] = send(
+                    parts[k].at[pl.ds(start, size)],
+                    from_core[k].at[pl.ds(j * size, size)],
+                    core_send.at[k, j],
+                    core_recv.at[k, j],
+                    sibling,
+                )
+    core_copies[last, 0].wait_recv()
+    small_pair[...] = small[...] + small_core[...]
+    side_copies[last, 0] = send(
+        small_pair, small_side, side_send.at[last, 0], side_recv.at[last, 0], side
+    )
+    for k in range(arrays):
+        size = sums[k].shape[0]
+        for d in order:
+            j = length + d
+            core_copies[k, j].wait_recv()
+            mine = part_start(k, d, 1 - column, core)
+            add_into((from_core[k], j * size), [(from_core[k], j * size), (parts[k], mine)], size)
+            side_copies[k, d] = send(
+                from_core[k].at[pl.ds(j * size, size)],
+                from_side[k].at[pl.ds(d * size, size)],
+                side_send.at[k, d],
+                side_recv.at[k, d],
+                side,
+            )
+    side_copies[last, 0].wait_recv()
+    small_line[line] = small_pair[...] + small_side[...]
+    for d in range(1, length):
+        line_copies[last, d] = send(
+            small_line.at[line],
+            small_line.at[line],
+            line_send.at[last, d],
+            line_recv.at[last, d],
+            ahead[d - 1],
+        )
+    for k in range(arrays):
+        size = sums[k].shape[0]
+        for d in order:
+            core_copies[k, d].wait_recv()
+            side_copies[k, d].wait_recv()
+            if d:
+                mine = part_start(k, d, column, core)
+                terms = [
+                    (from_side[k], d * size),
+                    (from_core[k], d * size),
+                    (parts[k], mine),
+                ]
+                add_into((from_side[k], d * size), terms, size)
+                line_copies[k, d] = send(
+                    from_side[k].at[pl.ds(d * size, size)],
+                    from_line[k].at[pl.ds((d - 1) * size, size)],
+                    line_send.at[k, d],
+                    line_recv.at[k, d],
+                    ahead[d - 1],
+                )
+    for d in range(1, length):
+        line_copies[last, d].wait_recv()
+    total = small_line[0]
+    for position in range(1, length):
+        total = total + small_line[position]
+    small_sum[...] = total
+    for k in range(arrays):
+        size = sums[k].shape[0]
+        terms = [
+            (from_side[k], 0),
+            (from_core[k], 0),
+            (parts[k], part_start(k, 0, column, core)),
+        ]
+        for d in range(1, length):
+            line_copies[k, d].wait_recv()
+            terms.append((from_line[k], (d - 1) * size))
+        add_into((sums[k], 0), terms, size)
+    for copies in (core_copies, side_copies, line_copies):
+        for copy in copies.values():
+            copy.wait_send()
+
+
+def scatter_rows(parts, small, count, collective_id):
+    size = parts[0].shape[0] // count
+    if size % 16 or count % 4:
+        sums = tuple(
+            lax.psum_scatter(
+                part.astype(jnp.float32), "dp", scatter_dimension=0, tiled=True
+            )
+            for part in parts
+        )
+        return sums + (lax.psum(small, "dp"),)
+    arrays, length = len(parts), count // 4
+    vmem = pl.BlockSpec(memory_space=pltpu.VMEM)
+    widths = [part.shape[1] for part in parts]
+    received = [
+        pltpu.VMEM((blocks * size, width), jnp.bfloat16)
+        for blocks in (2 * length, length, length - 1)
+        for width in widths
+    ]
+    return pl.pallas_call(
+        partial(scatter_kernel, count, arrays),
+        out_shape=tuple(jax.ShapeDtypeStruct((size, width), jnp.float32) for width in widths)
+        + (jax.ShapeDtypeStruct(small.shape, jnp.float32),),
+        in_specs=[vmem] * (arrays + 1),
+        out_specs=(vmem,) * (arrays + 1),
+        scratch_shapes=received
+        + [pltpu.VMEM(small.shape, jnp.float32)] * 3
+        + [pltpu.VMEM((length,) + small.shape, jnp.float32)]
+        + [pltpu.SemaphoreType.DMA((arrays + 1, 2 * length))] * 2
+        + [pltpu.SemaphoreType.DMA((arrays + 1, length))] * 4,
+        compiler_params=pltpu.CompilerParams(
+            collective_id=collective_id, has_side_effects=True, vmem_limit_bytes=VMEM_BYTES
+        ),
+    )(*parts, small)
+
+
+def exchange_kernel(arrays, pieces, *refs):
+    shares, totals = refs[:arrays], refs[arrays : 2 * arrays]
+    mine, theirs = refs[2 * arrays : 3 * arrays], refs[3 * arrays : 4 * arrays]
+    send_sem, recv_sem = refs[4 * arrays :]
+    peer = 1 - lax.axis_index("tensor")
+    barrier = pltpu.get_barrier_semaphore()
+    pl.semaphore_signal(barrier, inc=1, device_id={"tensor": peer}, device_id_type=MESH)
+    pl.semaphore_wait(barrier, 1)
+    copies = {}
+    for k in range(arrays):
+        size = shares[k].shape[0] // pieces[k]
+        for piece in range(pieces[k]):
+            at = pl.ds(piece * size, size)
+            mine[k][at, :] = shares[k][at, :].astype(jnp.bfloat16)
+            copies[k, piece] = pltpu.make_async_remote_copy(
+                src_ref=mine[k].at[at],
+                dst_ref=theirs[k].at[at],
+                send_sem=send_sem.at[k, piece],
+                recv_sem=recv_sem.at[k, piece],
+                device_id={"tensor": peer},
+                device_id_type=MESH,
+            )
+            copies[k, piece].start()
+    for k in range(arrays):
+        size = shares[k].shape[0] // pieces[k]
+        for piece in range(pieces[k]):
+            at = pl.ds(piece * size, size)
+            copies[k, piece].wait()
+            totals[k][at, :] = mine[k][at, :].astype(jnp.float32) + theirs[k][at, :].astype(
+                jnp.float32
+            )
+
+
+def tensor_sum(shares, ways, collective_id):
+    if ways != 2:
+        return tuple(lax.psum(share, "tensor") for share in shares)
+    arrays = len(shares)
+    pieces = tuple(4 if share.shape[0] % 64 == 0 else 1 for share in shares)
+    vmem = pl.BlockSpec(memory_space=pltpu.VMEM)
+    buffers = [pltpu.VMEM(share.shape, jnp.bfloat16) for share in shares]
+    return pl.pallas_call(
+        partial(exchange_kernel, arrays, pieces),
+        out_shape=tuple(jax.ShapeDtypeStruct(share.shape, jnp.float32) for share in shares),
+        in_specs=[vmem] * arrays,
+        out_specs=(vmem,) * arrays,
+        scratch_shapes=buffers + buffers + [pltpu.SemaphoreType.DMA((arrays, 4))] * 2,
+        compiler_params=pltpu.CompilerParams(
+            collective_id=collective_id, has_side_effects=True, vmem_limit_bytes=VMEM_BYTES
+        ),
+    )(*shares)
 
 
 def body(
@@ -176,37 +518,29 @@
     w_down,
     cotangent,
 ):
-    (
-        gain_in,
-        full_z,
-        full_x,
-        full_bc,
-        full_dt,
-        full_out,
-        full_q,
-        full_k,
-        full_v,
-        full_o,
-        gain_mlp,
-        full_gate,
-        full_up,
-        full_down,
-    ) = (
-        lax.all_gather(norm_in, "dp", axis=0, tiled=True),
-        lax.all_gather(w_z, "dp", axis=0, tiled=True),
-        lax.all_gather(w_x, "dp", axis=0, tiled=True),
-        lax.all_gather(w_bc, "dp", axis=0, tiled=True),
-        lax.all_gather(w_dt, "dp", axis=0, tiled=True),
-        lax.all_gather(w_out, "dp", axis=1, tiled=True),
-        lax.all_gather(w_q, "dp", axis=0, tiled=True),
-        lax.all_gather(key_weight, "dp", axis=0, tiled=True),
-        lax.all_gather(value_weight, "dp", axis=0, tiled=True),
-        lax.all_gather(w_o, "dp", axis=1, tiled=True),
-        lax.all_gather(norm_mlp, "dp", axis=0, tiled=True),
-        lax.all_gather(w_gate, "dp", axis=0, tiled=True),
-        lax.all_gather(w_up, "dp", axis=0, tiled=True),
-        lax.all_gather(w_down, "dp", axis=1, tiled=True),
-    )
+    count = lax.axis_size("dp")
+    ways = lax.axis_size("tensor")
+    width_z, width_bc, width_dt = w_z.shape[1], w_bc.shape[1], w_dt.shape[1]
+    width_q, width_k, width_o = w_q.shape[1], key_weight.shape[1], w_o.shape[0]
+    width_ff = w_gate.shape[1]
+    thin = jnp.concatenate([w_dt, norm_in[:, None], norm_mlp[:, None]], axis=1)
+    thin = jnp.pad(thin, ((0, 0), (0, -thin.shape[1] % 128)))
+    packed_in, packed_out, full_glu, down_t = gather_rows(
+        (
+            jnp.concatenate([w_z, w_x, w_bc, w_q, key_weight, value_weight, thin], axis=1),
+            jnp.concatenate([w_out.T, w_o.T], axis=1),
+            jnp.concatenate([w_gate, w_up], axis=1),
+            w_down.T,
+        ),
+        count,
+        0,
+    )
+    edges = [0]
+    for width in (width_z, width_z, width_bc, width_q, width_k, width_k, width_dt):
+        edges.append(edges[-1] + width)
+    gain_in = packed_in[:, edges[7]]
+    gain_mlp = packed_in[:, edges[7] + 1]
+    full_in = packed_in[:, : edges[7]]
     inputs = hidden_in.astype(jnp.float32)
     count_of_rows = inputs.shape[0]
     segment, token_position, live_rows = layout(seq_lengths, count_of_rows)
@@ -215,10 +549,10 @@
     visible = (segment[:, None] == segment[None, :]) & (row_index[None, :] <= row_index[:, None])
     normed_full, norm_in_pull = jax.vjp(root_norm, inputs, gain_in.astype(jnp.float32))
     normalized_input = normed_full.astype(jnp.bfloat16)
-    gate_ssm = product(normalized_input, full_z)
-    conv_in = product(normalized_input, full_x)
-    bc_raw = product(normalized_input, full_bc)
-    step_raw = product(normalized_input, full_dt)
+    projected = product(normalized_input, full_in)
+    gate_ssm, conv_in, bc_raw, q_raw, k_raw, v_raw, step_raw = (
+        projected[:, left:right] for left, right in zip(edges[:-1], edges[1:])
+    )
     bc_act, bc_pull = jax.vjp(
         partial(causal_conv, segment=segment), bc_raw, conv_bc.astype(jnp.float32)
     )
@@ -232,88 +566,53 @@
         bc_act,
     )
     gated_out = gated_full.astype(jnp.bfloat16)
-    query_heads = full_q.shape[1] // HEAD_WIDTH
-    kv_heads = full_k.shape[1] // HEAD_WIDTH
+    query_heads = width_q // HEAD_WIDTH
+    kv_heads = width_k // HEAD_WIDTH
     queries = rotary_embedding(
-        product(normalized_input, full_q).reshape(count_of_rows, query_heads, HEAD_WIDTH),
+        q_raw.reshape(count_of_rows, query_heads, HEAD_WIDTH),
         token_position,
         1.0,
     ).astype(jnp.bfloat16)
     key_matrix_rows = rotary_embedding(
-        product(normalized_input, full_k).reshape(count_of_rows, kv_heads, HEAD_WIDTH),
+        k_raw.reshape(count_of_rows, kv_heads, HEAD_WIDTH),
         token_position,
         1.0,
     ).astype(jnp.bfloat16)
     value_matrix_rows = (
-        product(normalized_input, full_v)
-        .astype(jnp.bfloat16)
+        v_raw.astype(jnp.bfloat16)
         .reshape(count_of_rows, kv_heads, HEAD_WIDTH)
     )
     attended_full, log_total = attend_forward(queries, key_matrix_rows, value_matrix_rows, visible)
     attended = attended_full.astype(jnp.bfloat16)
-    local_sum = product(gated_out, full_out) + product(attended, full_o)
-    mixed_sum = lax.psum(local_sum, "tensor")
+    mixed_in = jnp.concatenate([gated_out, attended], axis=1)
+    (mixed_sum,) = tensor_sum((back_product(mixed_in, packed_out),), ways, 1)
     residual = inputs + live_column * mixed_sum
     normed_mlp_full, norm_mlp_pull = jax.vjp(root_norm, residual, gain_mlp.astype(jnp.float32))
     normed_mlp = normed_mlp_full.astype(jnp.bfloat16)
-    gate_pre = product(normed_mlp, full_gate)
-    up_pre = product(normed_mlp, full_up)
+    glu_pre = product(normed_mlp, full_glu)
+    gate_pre, up_pre = glu_pre[:, :width_ff], glu_pre[:, width_ff:]
     activated = (jax.nn.silu(gate_pre) * up_pre).astype(jnp.bfloat16)
-    mlp_out = lax.psum(product(activated, full_down).astype(jnp.bfloat16), "tensor").astype(
-        jnp.float32
-    )
+    (mlp_out,) = tensor_sum((back_product(activated, down_t),), ways, 2)
     layer_out = residual + live_column * mlp_out
-    (
-        gain_in,
-        full_z,
-        full_x,
-        full_bc,
-        full_dt,
-        full_out,
-        full_q,
-        full_k,
-        full_v,
-        full_o,
-        gain_mlp,
-        full_gate,
-        full_up,
-        full_down,
-    ) = (
-        lax.all_gather(norm_in, "dp", axis=0, tiled=True),
-        lax.all_gather(w_z, "dp", axis=0, tiled=True),
-        lax.all_gather(w_x, "dp", axis=0, tiled=True),
-        lax.all_gather(w_bc, "dp", axis=0, tiled=True),
-        lax.all_gather(w_dt, "dp", axis=0, tiled=True),
-        lax.all_gather(w_out, "dp", axis=1, tiled=True),
-        lax.all_gather(w_q, "dp", axis=0, tiled=True),
-        lax.all_gather(key_weight, "dp", axis=0, tiled=True),
-        lax.all_gather(value_weight, "dp", axis=0, tiled=True),
-        lax.all_gather(w_o, "dp", axis=1, tiled=True),
-        lax.all_gather(norm_mlp, "dp", axis=0, tiled=True),
-        lax.all_gather(w_gate, "dp", axis=0, tiled=True),
-        lax.all_gather(w_up, "dp", axis=0, tiled=True),
-        lax.all_gather(w_down, "dp", axis=1, tiled=True),
-    )
     grad_out = cotangent.astype(jnp.float32)
     grad_mlp = (live_column * grad_out).astype(jnp.bfloat16)
-    grad_act = back_product(grad_mlp, full_down)
+    grad_act = product(grad_mlp, down_t)
     sigmoid_gate = jax.nn.sigmoid(gate_pre)
     grad_gate = (grad_act * up_pre * sigmoid_gate * (1.0 + gate_pre * (1.0 - sigmoid_gate))).astype(
         jnp.bfloat16
     )
     grad_up = (grad_act * jax.nn.silu(gate_pre)).astype(jnp.bfloat16)
-    part_down = rows_product(activated, grad_mlp)
-    part_gate = rows_product(normed_mlp, grad_gate)
-    part_up = rows_product(normed_mlp, grad_up)
-    mlp_norm_part = back_product(grad_gate, full_gate) + back_product(grad_up, full_up)
-    grad_normed_mlp = lax.psum(mlp_norm_part, "tensor")
+    grad_glu = jnp.concatenate([grad_gate, grad_up], axis=1)
+    part_down = rows_product(grad_mlp, activated).astype(jnp.bfloat16)
+    part_glu = rows_product(normed_mlp, grad_glu).astype(jnp.bfloat16)
+    (grad_normed_mlp,) = tensor_sum((back_product(grad_glu, full_glu),), ways, 3)
     grad_residual_norm, part_gain_mlp = norm_mlp_pull(grad_normed_mlp)
     grad_residual = grad_out + grad_residual_norm
     grad_mixed = (live_column * grad_residual).astype(jnp.bfloat16)
-    grad_gated = back_product(grad_mixed, full_out)
-    grad_attended = back_product(grad_mixed, full_o).astype(jnp.bfloat16)
-    part_out = rows_product(gated_out, grad_mixed)
-    part_o = rows_product(attended, grad_mixed)
+    grad_mixed_in = product(grad_mixed, packed_out)
+    grad_gated = grad_mixed_in[:, :width_z]
+    grad_attended = grad_mixed_in[:, width_z:].astype(jnp.bfloat16)
+    part_out = rows_product(grad_mixed, mixed_in).astype(jnp.bfloat16)
     grad_queries, grad_keys, grad_values = attend_backward(
         queries, key_matrix_rows, value_matrix_rows, visible, log_total, grad_attended
     )
@@ -331,67 +630,78 @@
     grad_gate_ssm, grad_conv_in, grad_step, part_conv_x, part_heads, bc_share = mamba_pull(
         grad_gated
     )
-    grad_bc_act = lax.psum(bc_share, "tensor")
-    grad_bc_raw, part_conv_bc = bc_pull(grad_bc_act)
+    bc_raw_share, conv_bc_share = bc_pull(bc_share)
     grad_gate_ssm = grad_gate_ssm.astype(jnp.bfloat16)
     grad_conv_in = grad_conv_in.astype(jnp.bfloat16)
     grad_step = grad_step.astype(jnp.bfloat16)
-    grad_bc_raw = grad_bc_raw.astype(jnp.bfloat16)
-    part_z = rows_product(normalized_input, grad_gate_ssm)
-    part_x = rows_product(normalized_input, grad_conv_in)
-    part_bc = rows_product(normalized_input, grad_bc_raw)
-    part_dt = rows_product(normalized_input, grad_step)
-    part_q = rows_product(normalized_input, grad_q)
-    part_k = rows_product(normalized_input, grad_k)
-    part_v = rows_product(normalized_input, grad_v)
-    share_weight = 1.0 / lax.axis_size("tensor")
-    norm_part = (
-        back_product(grad_gate_ssm, full_z)
-        + back_product(grad_conv_in, full_x)
-        + back_product(grad_step, full_dt)
-    )
-    norm_part = norm_part + back_product(grad_bc_raw, full_bc) * share_weight
-    norm_part = (
-        norm_part
-        + back_product(grad_q, full_q)
-        + back_product(grad_k, full_k)
-        + back_product(grad_v, full_v)
-    )
-    grad_normed = lax.psum(norm_part.astype(jnp.bfloat16), "tensor").astype(jnp.float32)
+    grad_projected = jnp.concatenate(
+        [
+            grad_gate_ssm,
+            grad_conv_in,
+            bc_raw_share.astype(jnp.bfloat16),
+            grad_q,
+            grad_k,
+            grad_v,
+            grad_step,
+        ],
+        axis=1,
+    )
+    conv_rows = conv_bc.shape[0]
+    bc_terms = jnp.concatenate(
+        [bc_raw_share, jnp.pad(conv_bc_share, ((0, -conv_rows % 16), (0, 0)))], axis=0
+    )
+    grad_normed, bc_sums = tensor_sum(
+        (back_product(grad_projected, full_in), bc_terms), ways, 4
+    )
+    grad_bc_raw = bc_sums[:count_of_rows].astype(jnp.bfloat16)
+    part_conv_bc = bc_sums[count_of_rows : count_of_rows + conv_rows]
     grad_input_norm, part_gain_in = norm_in_pull(grad_normed)
     grad_in = grad_residual + grad_input_norm
-    sum_conv_x, sum_conv_bc, sum_heads = lax.psum((part_conv_x, part_conv_bc, part_heads), "dp")
-    (
-        sum_gain_in,
-        sum_z,
-        sum_x,
-        sum_bc,
-        sum_dt,
-        sum_out,
-        sum_q,
-        sum_k,
-        sum_v,
-        sum_o,
-        sum_gain_mlp,
-        sum_gate,
-        sum_up,
-        sum_down,
-    ) = (
-        lax.psum_scatter(part_gain_in, "dp", scatter_dimension=0, tiled=True),
-        lax.psum_scatter(part_z, "dp", scatter_dimension=0, tiled=True),
-        lax.psum_scatter(part_x, "dp", scatter_dimension=0, tiled=True),
-        lax.psum_scatter(part_bc, "dp", scatter_dimension=0, tiled=True),
-        lax.psum_scatter(part_dt, "dp", scatter_dimension=0, tiled=True),
-        lax.psum_scatter(part_out, "dp", scatter_dimension=1, tiled=True),
-        lax.psum_scatter(part_q, "dp", scatter_dimension=0, tiled=True),
-        lax.psum_scatter(part_k, "dp", scatter_dimension=0, tiled=True),
-        lax.psum_scatter(part_v, "dp", scatter_dimension=0, tiled=True),
-        lax.psum_scatter(part_o, "dp", scatter_dimension=1, tiled=True),
-        lax.psum_scatter(part_gain_mlp, "dp", scatter_dimension=0, tiled=True),
-        lax.psum_scatter(part_gate, "dp", scatter_dimension=0, tiled=True),
-        lax.psum_scatter(part_up, "dp", scatter_dimension=0, tiled=True),
-        lax.psum_scatter(part_down, "dp", scatter_dimension=1, tiled=True),
-    )
+    grad_projected = jnp.concatenate(
+        [
+            grad_gate_ssm,
+            grad_conv_in,
+            grad_bc_raw,
+            grad_q,
+            grad_k,
+            grad_v,
+            grad_step,
+        ],
+        axis=1,
+    )
+    part_in = jnp.concatenate(
+        [
+            rows_product(normalized_input, grad_projected),
+            part_gain_in[:, None],
+            part_gain_mlp[:, None],
+        ],
+        axis=1,
+    ).astype(jnp.bfloat16)
+    part_in = jnp.pad(part_in, ((0, 0), (0, packed_in.shape[1] - part_in.shape[1])))
+    head_rows, head_count = head_params.shape
+    small = jnp.concatenate(
+        [
+            jnp.pad(part_conv_x, ((0, 8 - conv_rows), (0, 0))),
+            jnp.pad(part_conv_bc, ((0, 8 - conv_rows), (0, 0))),
+            jnp.pad(part_heads, ((0, 8 - head_rows), (0, -head_count % 128))),
+        ],
+        axis=1,
+    )
+    sum_in, sum_out_o, sum_glu, sum_down, sum_small = scatter_rows(
+        (part_in, part_out, part_glu, part_down), small, count, 5
+    )
+    sum_z, sum_x, sum_bc, sum_q, sum_k, sum_v, sum_dt = (
+        sum_in[:, left:right] for left, right in zip(edges[:-1], edges[1:])
+    )
+    sum_gain_in = sum_in[:, edges[7]]
+    sum_gain_mlp = sum_in[:, edges[7] + 1]
+    sum_out = sum_out_o[:, :width_z].T
+    sum_o = sum_out_o[:, width_z:].T
+    sum_gate, sum_up = sum_glu[:, :width_ff], sum_glu[:, width_ff:]
+    sum_down = sum_down.T
+    sum_conv_x = sum_small[:conv_rows, :width_z]
+    sum_conv_bc = sum_small[:conv_rows, width_z : width_z + width_bc]
+    sum_heads = sum_small[:head_rows, width_z + width_bc : width_z + width_bc + head_count]
     return (
         layer_out,
         grad_in,

time: 1330 us -> 410 us (0.31)
  waiting for transfers between devices: 950 us -> 0 us
  Pallas kernels: 0 us -> 244 us
  blocking collectives: 198 us -> 0 us
  matrix products: 86.5 us -> 45.9 us
  local copies, waits for them, and re-layouts: 22.9 us -> 60.9 us
  between operations: 17.6 us -> 2.96 us
    reduce_scatter x11 -> x0, waiting for transfers between devices: 681 us -> none  [the longest x1 76.4 us: body(): lax.psum_scatter(part_up, 'dp', scatter_dimension=0, tiled=True)]
    pallas_call x0 -> x6, Pallas kernels: none -> 244 us  [the longest x1 95.9 us: scatter_rows(): pl.pallas_call(partial(scatter_kernel, count, arrays), out_shape=tuple((j...]
    all_gather x6 -> x0, blocking collectives: 125 us -> none  [the longest x1 26.3 us: body(): lax.all_gather(w_dt, 'dp', axis=0, tiled=True)]
    psum x4 -> x0, waiting for transfers between devices: 123 us -> none  [the longest x1 42.7 us: body(): lax.psum(product(activated, full_down).astype(jnp.bfloat16), 'tensor')]
    all_gather x6 -> x0, waiting for transfers between devices: 120 us -> none  [the longest x1 41.4 us: body(): lax.all_gather(w_up, 'dp', axis=0, tiled=True)]
    unnamed x2 -> x0, blocking collectives: 72.3 us -> none
    unnamed x23 -> x0, waiting for transfers between devices: 26.6 us -> none
    dot_general x12 -> x4, matrix products: 23.2 us -> 7.53 us  [product(): return jnp.dot(left_side, right_side, preferred_element_type=jnp.float32)]
  transfers between devices with their start and end apart: 22 -> 0, of which waited for: 19 -> 0; matrix products, arithmetic and copies ran while one was open for 8% -> 0% of each run, Pallas kernels for 0% -> 0%
where the time goes in v1:
time: 410 us; the launch traced here: 402 us
  Pallas kernels  244 us (60%)
  local copies, waits for them, and re-layouts  60.9 us (15%)
  other arithmetic  48.6 us (12%)
  matrix products  45.9 us (11%)
    pallas_call x1, Pallas kernels, scatter_rows(): pl.pallas_call(partial(scatter_kernel, count, arrays), out_shape=tuple((j...  95.9 us
    pallas_call x1, Pallas kernels, gather_rows(): pl.pallas_call(partial(gather_kernel, count, arrays), out_shape=tuple((ja...  91.6 us
    pallas_call x4, Pallas kernels, tensor_sum(): pl.pallas_call(partial(exchange_kernel, arrays, pieces), out_shape=tuple(...  56.6 us
    unnamed x267, local copies, waits for them, and re-layouts  14.5 us
    dot_general x3, matrix products, state_mix(): result = jnp.einsum('hts,shp->thp', mixing, inputs, precision=EXACT_PRODUCT)  12 us
    dot_general x4, matrix products, rows_product(): lax.dot_general(left_side, right_side, (((0,), (0,)), ((), ())), preferre...  11.6 us
    another operation x11, other arithmetic  8.99 us
    another operation x8, local copies, waits for them, and re-layouts  8.76 us

profile of v1, /device:TPU:9, one launch (start us, length us, event | category | flops | bytes accessed | tf_op | source)
XLA Modules:
  0.0 402.4 jit_solution(10770046102817178300)
XLA Ops:
  0.7 0.9 reduce-window.16
  2.2 1.2 compare_convert_fusion.3
  3.5 1.2 fusion.46
  5.5 1.3 slice_bitcast_fusion.3
  8.2 1.5 fusion.138
  12.8 1.6 pad_maximum_fusion.7.refs_1_
  14.4 1.7 pad_maximum_fusion.6.refs_2_
  16.1 1.8 concatenate.96.refs_0_
  17.9 91.6 %shard_map.339 = (bf16[1024,2304]{1,0:T(8,128)(2,1)}, bf16[1024,1024]{1,0:T(8,128)(2,1)}, bf16[1024,2048]{1,0:T(8,128)(2,1)}, bf16[1024,1024]{1,0:T(8,128)(2,1)}) custom-call(bf16[64,2304]{1,0:T(8,128)(2,1)} %concatenate.96.refs_0_, bf16[64,1024]{1,0:T(8,128)(2,1)} %pad_maximum_fusion.7.refs_1_, bf16[64,2048]{1,0:T(8,128)(2,1)} %pad_maximum_fusion.6.refs_2_, ...), custom_call_target="tpu_custom_call" | custom-call | tf_op jit(solution)/shard_map/pallas_call | solution.py:259
  109.4 2.1 convert_reduce_fusion
  111.5 4.3 %fusion.2 = f32[256,2188]{0,1:T(8,128)S(1)} fusion(bf16[1024,2304]{1,0:T(8,128)(2,1)} %get-tuple-element.30, bf16[256,1024]{1,0:T(8,128)(2,1)S(1)} %copy-done.5, f32[1024]{0:T(1024)S(1)} %get-tuple-element.137, f32[256]{0:T(256)S(1)} %fusion.112), kind=kOutput, calls=%fused_computation.3 | convolution fusion | flops 1148190720 | bytes 7488512 | tf_op jit(solution)/shard_map/dot_general | solution.py:20
  120.3 1.1 copy.154
  121.4 0.9 subtract_convert_fusion.1
  122.3 1.7 fusion.68
  127.0 2.3 fusion.58
  129.3 0.9 copy-done.37
  130.2 3.6 fusion.34
  135.5 1.7 fusion.65.refs_0_
  137.2 14.9 %shard_map.340 = f32[256,1024]{1,0:T(8,128)S(1)} custom-call(f32[256,1024]{1,0:T(8,128)} %fusion.65.refs_0_), custom_call_target="tpu_custom_call" | custom-call | tf_op jit(solution)/shard_map/pallas_call | solution.py:487
  152.5 1.3 fusion.126
  154.1 1.2 multiply_convert_fusion.3
  155.3 1.8 fusion.140.refs_0_
  157.1 2.3 fusion.59.refs_0_
  159.4 13.8 %shard_map.342 = f32[256,1024]{1,0:T(8,128)S(1)} custom-call(f32[256,1024]{1,0:T(8,128)} %fusion.59.refs_0_), custom_call_target="tpu_custom_call" | custom-call | tf_op jit(solution)/shard_map/pallas_call | solution.py:487
  173.2 12.9 %shard_map.341 = f32[256,1024]{1,0:T(8,128)S(1)} custom-call(f32[256,1024]{1,0:T(8,128)} %fusion.140.refs_0_), custom_call_target="tpu_custom_call" | custom-call | tf_op jit(solution)/shard_map/pallas_call | solution.py:487
  186.9 1.4 convert_add_fusion.1
  188.3 1.0 copy-done.1
  190.7 1.0 slice.321
  191.6 2.3 copy.158
  194.0 3.7 multiply_reduce_fusion.6
  197.7 5.5 %fusion.11 = (f32[12,256]{1,0:T(8,128)S(1)}, f32[12,256]{1,0:T(8,128)S(1)}, f32[12,256]{1,0:T(8,128)}, f32[256,256]{1,0:T(8,128)}) fusion(f32[12,256]{1,0:T(8,128)S(1)} %copy-done.103, f32[12,256]{1,0:T(8,128)S(1)} %bitcast.208, f32[256,256]{1,0:T(8,128)S(1)} %copy-done.49, pred[256,256]{1,0:T(8,128)(4,1)S(1)} %copy-done.75, ...), kind=kOutput, calls=%fused_computation.22 | convolution fusion | flops 614128640 | bytes 2224128 | tf_op jit(solution)/shard_map/transpose(jvp(hts,shp->thp))/dot_general | solution.py:96
  203.8 1.3 add_any.101
  205.1 1.7 copy.138
  206.8 1.3 reduce_sum.293
  208.1 1.3 reduce_sum.294
  209.5 1.3 copy.142
  210.8 4.0 reduce-window.21
  214.7 1.4 slice_reduce_fusion.2
  216.1 1.3 reduce-window.24
  219.0 1.5 fusion.129
  221.2 1.2 pad_add_fusion.2
  222.4 1.4 fusion.75
  223.8 1.6 fusion.79
  225.4 1.2 multiply_reduce_fusion.14
  226.9 0.9 broadcast_in_dim.74
  228.3 2.8 fusion.31
  234.6 1.8 multiply_reduce_fusion.7
  236.4 1.2 multiply_reduce_fusion.3
  239.6 1.0 copy.167
  240.7 0.9 constant_dynamic-update-slice_fusion.1
  241.7 2.5 fusion.refs_0_
  244.2 15.1 %shard_map.343 = (f32[256,1024]{1,0:T(8,128)S(1)}, f32[272,256]{1,0:T(8,128)S(1)}) custom-call(f32[256,1024]{1,0:T(8,128)} %fusion.refs_0_, f32[272,256]{1,0:T(8,128)S(1)} %select_maximum_fusion.refs_1_), custom_call_target="tpu_custom_call" | custom-call | tf_op jit(solution)/shard_map/pallas_call | solution.py:487
  259.3 0.9 fusion.43
  260.3 1.3 fusion.45
  262.2 1.0 copy.145
  267.1 0.9 broadcast_in_dim.73
  268.0 2.5 convolution_convert_fusion.3.refs_1_
  270.5 2.2 convolution_convert_fusion.2.refs_3_
  272.7 3.5 convolution_convert_fusion.1.refs_2_
  276.2 3.6 convolution_convert_fusion
  279.7 6.6 %copy.146 = bf16[1024,2188]{1,0:T(8,128)(2,1)} copy(bf16[1024,2188]{0,1:T(8,128)(2,1)} %convolution_convert_fusion) | data formatting | bytes 8962048 | tf_op jit(solution)/shard_map/convert.2
  286.4 8.0 %concatenate.119 = bf16[1024,2190]{1,0:T(8,128)(2,1)} concatenate(bf16[1024,2188]{1,0:T(8,128)(2,1)} %copy.146, bf16[1024,1]{1,0:T(8,128)(2,1)S(1)} %broadcast_in_dim.73, bf16[1024,1]{1,0:T(8,128)(2,1)S(1)} %copy-done.34), dimensions={1} | concatenate | bytes 8970240 | tf_op jit(solution)/shard_map/concatenate | solution.py:672
  294.3 4.9 %pad.110.refs_0_ = bf16[1024,2304]{1,0:T(8,128)(2,1)} pad(bf16[1024,2190]{1,0:T(8,128)(2,1)} %concatenate.119, bf16[]{:T(256)} %constant.33.clone.1), padding=0_0x0_114 | pad | bytes 9203714 | tf_op jit(solution)/shard_map/jit(_pad)/pad | solution.py:680
  299.2 95.9 %shard_map.344 = (f32[64,2304]{1,0:T(8,128)S(1)}, f32[64,1024]{1,0:T(8,128)S(1)}, f32[64,2048]{1,0:T(8,128)S(1)}, f32[64,1024]{1,0:T(8,128)S(1)}, f32[8,1152]{1,0:T(8,128)S(1)}) custom-call(bf16[1024,2304]{1,0:T(8,128)(2,1)} %pad.110.refs_0_, bf16[1024,1024]{1,0:T(8,128)(2,1)} %convolution_convert_fusion.3.refs_1_, ...), custom_call_target="tpu_custom_call" | custom-call | tf_op jit(solution)/shard_map/pallas_call | solution.py:430
  (355 shorter events, 37.8 us)
Async XLA Ops:
  0.7 110.8 %copy-start.5 = (bf16[256,1024]{1,0:T(8,128)(2,1)S(1)}, bf16[256,1024]{1,0:T(8,128)(2,1)}, u32[]{:S(2)}) copy-start(bf16[256,1024]{1,0:T(8,128)(2,1)} %param.20) | copy-start | bytes 1572868
  0.7 117.5 %copy-start.116 = (f32[32]{0:T(128)}, f32[32]{0:T(128)S(1)}, u32[]{:S(2)}) copy-start(f32[32]{0:T(128)S(1)} %multiply_power_fusion) | copy-start | bytes 388
  4.7 5.0 %copy-start.113 = (f32[256]{0:T(256)}, f32[256]{0:T(256)S(1)}, u32[]{:S(2)}) copy-start(f32[256]{0:T(256)S(1)} %fusion.46) | copy-start | bytes 3076
  4.7 111.1 %copy-start.97 = (f32[256]{0:T(256)}, f32[256]{0:T(256)S(1)}, u32[]{:S(2)}) copy-start(f32[256]{0:T(256)S(1)} %fusion.112) | copy-start | bytes 3076
  5.5 112.8 %copy-start.100 = (f32[256]{0:T(256)}, f32[256]{0:T(256)S(1)}, u32[]{:S(2)}) copy-start(f32[256]{0:T(256)S(1)} %subtract_convert_fusion.2) | copy-start | bytes 3076
  6.8 109.0 %copy-start.118 = (f32[12]{0:T(128)}, f32[12]{0:T(128)S(1)}, u32[]{:S(2)}) copy-start(f32[12]{0:T(128)S(1)} %get-tuple-element.223) | copy-start | bytes 148
  6.8 109.1 %copy-start.119 = (f32[12]{0:T(128)}, f32[12]{0:T(128)S(1)}, u32[]{:S(2)}) copy-start(f32[12]{0:T(128)S(1)} %get-tuple-element.224) | copy-start | bytes 148
  11.2 104.6 %copy-start.51 = (pred[256,256]{0,1:T(8,128)(4,1)}, pred[256,256]{0,1:T(8,128)(4,1)S(1)}, u32[]{:S(2)}) copy-start(pred[256,256]{0,1:T(8,128)(4,1)S(1)} %fusion.69) | copy-start | bytes 196612
  111.5 4.4 %copy-start.57 = (f32[1024]{0:T(1024)}, f32[1024]{0:T(1024)S(1)}, u32[]{:S(2)}) copy-start(f32[1024]{0:T(1024)S(1)} %get-tuple-element.137) | copy-start | bytes 12292
  115.9 103.1 %copy-start = (f32[256,2188]{0,1:T(8,128)}, f32[256,2188]{0,1:T(8,128)S(1)}, u32[]{:S(2)}) copy-start(f32[256,2188]{0,1:T(8,128)S(1)} %fusion.2) | copy-start | bytes 6721540
  119.4 4.6 %copy-start.21 = (f32[255,256]{1,0:T(8,128)}, f32[255,256]{1,0:T(8,128)S(1)}, u32[]{:S(2)}) copy-start(f32[255,256]{1,0:T(8,128)S(1)} %copy.155) | copy-start | bytes 783364
  119.5 5.0 %copy-start.23 = (f32[253,256]{1,0:T(8,128)}, f32[253,256]{1,0:T(8,128)S(1)}, u32[]{:S(2)}) copy-start(f32[253,256]{1,0:T(8,128)S(1)} %copy.157) | copy-start | bytes 777220
  121.4 3.2 copy-start.24
  124.4 4.9 %copy-start.48 = (f32[256,256]{1,0:T(8,128)}, f32[256,256]{1,0:T(8,128)S(1)}, u32[]{:S(2)}) copy-start(f32[256,256]{1,0:T(8,128)S(1)} %fusion.77) | copy-start | bytes 786436
  126.8 7.2 %copy-start.43 = (bf16[64,4,256]{2,0,1:T(8,128)(2,1)}, bf16[64,4,256]{2,0,1:T(8,128)(2,1)S(1)}, u32[]{:S(2)}) copy-start(bf16[64,4,256]{2,0,1:T(8,128)(2,1)S(1)} %convolution_convert_fusion.4) | copy-start | bytes 393220
  126.9 3.2 copy-start.74
  127.0 3.2 copy-start.102
  127.0 3.2 copy-start.105
  127.0 3.2 copy-start.120
  130.2 5.3 %copy-start.8 = (bf16[1024,1024]{1,0:T(8,128)(2,1)S(1)}, bf16[1024,1024]{1,0:T(8,128)(2,1)}, u32[]{:S(2)}) copy-start(bf16[1024,1024]{1,0:T(8,128)(2,1)} %get-tuple-element.31) | copy-start | bytes 6291460
  135.5 16.6 %copy-start.6 = (bf16[256,1024]{1,0:T(8,128)(2,1)S(1)}, bf16[256,1024]{1,0:T(8,128)(2,1)}, u32[]{:S(2)}) copy-start(bf16[256,1024]{1,0:T(8,128)(2,1)} %param.20) | copy-start | bytes 1572868
  135.5 16.6 %copy-start.77 = (f32[256]{0:T(256)S(1)}, f32[256]{0:T(256)}, u32[]{:S(2)}) copy-start(f32[256]{0:T(256)} %compare_convert_fusion.3) | copy-start | bytes 3076
  137.2 15.2 %copy-start.17 = (bf16[1024,2048]{1,0:T(8,128)(2,1)S(1)}, bf16[1024,2048]{1,0:T(8,128)(2,1)}, u32[]{:S(2)}) copy-start(bf16[1024,2048]{1,0:T(8,128)(2,1)} %get-tuple-element.32) | copy-start | bytes 12582916
  137.2 15.2 %copy-start.46 = (f32[1024]{0:T(1024)S(1)}, f32[1024]{0:T(1024)}, u32[]{:S(2)}) copy-start(f32[1024]{0:T(1024)} %get-tuple-element.136) | copy-start | bytes 12292
  152.5 34.4 %copy-start.79 = (f32[256]{0:T(256)}, f32[256]{0:T(256)S(1)}, u32[]{:S(2)}) copy-start(f32[256]{0:T(256)S(1)} %fusion.113) | copy-start | bytes 3076
  155.3 4.1 %copy-start.30 = (bf16[256,1024]{1,0:T(8,128)(2,1)}, bf16[256,1024]{1,0:T(8,128)(2,1)S(1)}, u32[]{:S(2)}) copy-start(bf16[256,1024]{1,0:T(8,128)(2,1)S(1)} %get-tuple-element.191) | copy-start | bytes 1572868
  193.9 3.7 copy-start.38
  193.9 3.7 copy-start.49
  193.9 3.7 copy-start.75
  193.9 3.7 copy-start.103
  193.9 3.7 copy-start.106
  197.6 5.6 %copy-start.35 = (f32[256,768]{0,1:T(8,128)}, f32[256,768]{0,1:T(8,128)S(1)}, u32[]{:S(2)}) copy-start(f32[256,768]{0,1:T(8,128)S(1)} %get-tuple-element.165) | copy-start | bytes 2359300
  217.4 9.2 %copy-start.22 = (f32[255,256]{1,0:T(8,128)S(1)}, f32[255,256]{1,0:T(8,128)}, u32[]{:S(2)}) copy-start(f32[255,256]{1,0:T(8,128)} %copy-done.21) | copy-start | bytes 783364
  217.4 9.2 %copy-start.90 = (f32[256]{0:T(256)S(1)}, f32[256]{0:T(256)}, u32[]{:S(2)}) copy-start(f32[256]{0:T(256)} %get-tuple-element.228) | copy-start | bytes 3076
  217.4 9.2 %copy-start.93 = (f32[256]{0:T(256)S(1)}, f32[256]{0:T(256)}, u32[]{:S(2)}) copy-start(f32[256]{0:T(256)} %get-tuple-element.230) | copy-start | bytes 3076
  217.4 9.5 %copy-start.115 = (bf16[1024]{0:T(1024)(128)(2,1)S(1)}, bf16[1024]{0:T(1024)(128)(2,1)}, u32[]{:S(2)}) copy-start(bf16[1024]{0:T(1024)(128)(2,1)} %get-tuple-element.142) | copy-start | bytes 6148
  217.4 10.4 %copy-start.112 = (f32[1,256]{1,0:T(1,128)S(1)}, f32[1,256]{1,0:T(1,128)}, u32[]{:S(2)}) copy-start(f32[1,256]{1,0:T(1,128)} %get-tuple-element.220) | copy-start | bytes 3076
  221.2 6.7 %copy-start.111 = (f32[1,256]{1,0:T(1,128)S(1)}, f32[1,256]{1,0:T(1,128)}, u32[]{:S(2)}) copy-start(f32[1,256]{1,0:T(1,128)} %get-tuple-element.219) | copy-start | bytes 3076
  223.8 4.1 %copy-start.110 = (f32[1,256]{1,0:T(1,128)S(1)}, f32[1,256]{1,0:T(1,128)}, u32[]{:S(2)}) copy-start(f32[1,256]{1,0:T(1,128)} %get-tuple-element.221) | copy-start | bytes 3076
  225.4 2.6 copy-start.25
  228.3 2.8 copy-start.9
  228.3 2.8 copy-start.15
  228.3 2.8 copy-start.96
  234.6 7.1 %slice-start = ((s8[4718592]{0:T(1024)(128)(4,1)}), s8[4194304]{0:T(1024)(128)(4,1)S(1)}, s32[]{:S(2)}) async-start(s8[4718592]{0:T(1024)(128)(4,1)} %bitcast.201), calls=%async_computation | async-start | bytes 8388608
  237.7 4.0 slice-start.1
  241.7 17.6 %copy-start.7 = (bf16[256,1024]{1,0:T(8,128)(2,1)S(1)}, bf16[256,1024]{1,0:T(8,128)(2,1)}, u32[]{:S(2)}) copy-start(bf16[256,1024]{1,0:T(8,128)(2,1)} %param.20) | copy-start | bytes 1572868
  241.7 17.6 %copy-start.58 = (f32[1024]{0:T(1024)S(1)}, f32[1024]{0:T(1024)}, u32[]{:S(2)}) copy-start(f32[1024]{0:T(1024)} %copy-done.57) | copy-start | bytes 12292
  241.7 17.6 %copy-start.98 = (f32[256]{0:T(256)S(1)}, f32[256]{0:T(256)}, u32[]{:S(2)}) copy-start(f32[256]{0:T(256)} %copy-done.97) | copy-start | bytes 3076
  244.2 16.0 %copy-start.114 = (f32[256]{0:T(256)S(1)}, f32[256]{0:T(256)}, u32[]{:S(2)}) copy-start(f32[256]{0:T(256)} %copy-done.113) | copy-start | bytes 3076
  244.2 16.1 %copy-start.2 = (f32[256,1024]{1,0:T(8,128)S(1)}, f32[256,1024]{1,0:T(8,128)}, u32[]{:S(2)}) copy-start(f32[256,1024]{1,0:T(8,128)} %copy-done.1) | copy-start | bytes 3145732
  260.2 4.4 %copy-start.61 = (bf16[256,1,32]{0,2,1:T(8,128)(2,1)S(1)}, bf16[256,1,32]{0,2,1:T(8,128)(2,1)}, u32[]{:S(2)}) copy-start(bf16[256,1,32]{0,2,1:T(8,128)(2,1)} %copy-done.60) | copy-start | bytes 49156
  260.2 4.4 %copy-start.63 = (bf16[256,1,32]{0,2,1:T(8,128)(2,1)S(1)}, bf16[256,1,32]{0,2,1:T(8,128)(2,1)}, u32[]{:S(2)}) copy-start(bf16[256,1,32]{0,2,1:T(8,128)(2,1)} %copy-done.62) | copy-start | bytes 49156
  260.2 5.0 %copy-start.65 = (bf16[256,64]{0,1:T(8,128)(2,1)S(1)}, bf16[256,64]{0,1:T(8,128)(2,1)}, u32[]{:S(2)}) copy-start(bf16[256,64]{0,1:T(8,128)(2,1)} %get-tuple-element.236) | copy-start | bytes 98308
  260.2 5.6 %copy-start.68 = (bf16[256,12]{0,1:T(8,128)(2,1)S(1)}, bf16[256,12]{0,1:T(8,128)(2,1)}, u32[]{:S(2)}) copy-start(bf16[256,12]{0,1:T(8,128)(2,1)} %get-tuple-element.167) | copy-start | bytes 18436
  260.3 6.2 %copy-start.66 = (f32[5,768]{1,0:T(8,128)S(1)}, f32[5,768]{1,0:T(8,128)}, u32[]{:S(2)}) copy-start(f32[5,768]{1,0:T(8,128)} %pad_add_fusion) | copy-start | bytes 46084
  260.3 7.7 %copy-start.19 = (bf16[256,768]{0,1:T(8,128)(2,1)S(1)}, bf16[256,768]{0,1:T(8,128)(2,1)}, u32[]{:S(2)}) copy-start(bf16[256,768]{0,1:T(8,128)(2,1)} %copy-done.18) | copy-start | bytes 1179652
  260.3 7.7 %copy-start.44 = (bf16[64,4,256]{2,0,1:T(8,128)(2,1)S(1)}, bf16[64,4,256]{2,0,1:T(8,128)(2,1)}, u32[]{:S(2)}) copy-start(bf16[64,4,256]{2,0,1:T(8,128)(2,1)} %copy-done.43) | copy-start | bytes 393220
  260.3 7.7 %copy-start.78 = (f32[256]{0:T(256)S(1)}, f32[256]{0:T(256)}, u32[]{:S(2)}) copy-start(f32[256]{0:T(256)} %compare_convert_fusion.3) | copy-start | bytes 3076
  263.9 6.6 %copy-start.29 = (bf16[256,1024]{1,0:T(8,128)(2,1)S(1)}, bf16[256,1024]{1,0:T(8,128)(2,1)}, u32[]{:S(2)}) copy-start(bf16[256,1024]{1,0:T(8,128)(2,1)} %param.39) | copy-start | bytes 1572868
  263.9 6.6 %copy-start.31 = (bf16[256,1024]{1,0:T(8,128)(2,1)S(1)}, bf16[256,1024]{1,0:T(8,128)(2,1)}, u32[]{:S(2)}) copy-start(bf16[256,1024]{1,0:T(8,128)(2,1)} %copy-done.30) | copy-start | bytes 1572868
  272.7 3.5 copy-start.16
  272.7 3.5 copy-start.59
  272.7 3.5 copy-start.99
  279.7 6.6 %copy-start.34 = (bf16[1024,1]{1,0:T(8,128)(2,1)S(1)}, bf16[1024,1]{1,0:T(8,128)(2,1)}, u32[]{:S(2)}) copy-start(bf16[1024,1]{1,0:T(8,128)(2,1)} %broadcast_in_dim.74) | copy-start | bytes 6148
  (60 other events, 85.4 us)

commit v2 on v1

--- a/solution.py
+++ b/solution.py
@@ -173,11 +173,13 @@
     return (line * 2 + column) * 2 + core
 
 
-def greet(peers):
+def greet(peers, partner=None):
     barrier = pltpu.get_barrier_semaphore()
+    if partner is not None:
+        pl.semaphore_signal(barrier, inc=1, device_id={"tensor": partner}, device_id_type=MESH)
     for peer in peers:
         pl.semaphore_signal(barrier, inc=1, device_id={"dp": peer}, device_id_type=MESH)
-    pl.semaphore_wait(barrier, len(peers))
+    pl.semaphore_wait(barrier, len(peers) + (partner is not None))
 
 
 def gather_kernel(count, arrays, *refs):
@@ -270,10 +272,15 @@
     )(*shards)
 
 
-def scatter_kernel(count, arrays, *refs):
+def scatter_kernel(count, arrays, pairs, paired, paired_small, *refs):
     parts, small = refs[:arrays], refs[arrays]
-    sums, small_sum = refs[arrays + 1 : 2 * arrays + 1], refs[2 * arrays + 1]
-    rest = refs[2 * arrays + 2 :]
+    shares, refs = refs[arrays + 1 : arrays + 1 + pairs], refs[arrays + 1 + pairs :]
+    sums, small_sum = refs[:arrays], refs[arrays]
+    totals, rest = refs[arrays + 1 : arrays + 1 + pairs], refs[arrays + 1 + pairs :]
+    theirs, rest = rest[:pairs], rest[pairs:]
+    pair_in, pair_small, pair_send, pair_recv = rest[:4]
+    rest = rest[4:]
+    partner = 1 - lax.axis_index("tensor")
     from_core, from_side, from_line = (
         rest[:arrays],
         rest[arrays : 2 * arrays],
@@ -285,7 +292,19 @@
     side = dp_index(line, 1 - column, core)
     sibling = dp_index(line, column, 1 - core)
     ahead = [dp_index(lax.rem(line + d, length), column, core) for d in range(1, length)]
-    greet(ahead + [side, sibling])
+    greet(ahead + [side, sibling], partner)
+
+    def swap(source, target, index):
+        copy = pltpu.make_async_remote_copy(
+            src_ref=source,
+            dst_ref=target,
+            send_sem=pair_send.at[index],
+            recv_sem=pair_recv.at[index],
+            device_id={"tensor": partner},
+            device_id_type=MESH,
+        )
+        copy.start()
+        return copy
 
     def send(source, target, send_sem, recv_sem, peer):
         copy = pltpu.make_async_remote_copy(
@@ -320,43 +339,43 @@
 
     core_copies, side_copies, line_copies = {}, {}, {}
     last = arrays
-    order = list(range(1, length)) + [0]
     core_copies[last, 0] = send(
         small, small_core, core_send.at[last, 0], core_recv.at[last, 0], sibling
     )
+    far_first = [(k, d) for k in range(arrays) for d in range(1, length)]
+    far_first += [(k, 0) for k in range(arrays)]
     for other in (1, 0):
-        for k in range(arrays):
+        for k, d in far_first:
             size = sums[k].shape[0]
-            for d in order:
-                j = other * length + d
-                block_column = 1 - column if other else column
-                start = part_start(k, d, block_column, 1 - core)
-                core_copies[k, j] = send(
-                    parts[k].at[pl.ds(start, size)],
-                    from_core[k].at[pl.ds(j * size, size)],
-                    core_send.at[k, j],
-                    core_recv.at[k, j],
-                    sibling,
-                )
+            j = other * length + d
+            block_column = 1 - column if other else column
+            start = part_start(k, d, block_column, 1 - core)
+            core_copies[k, j] = send(
+                parts[k].at[pl.ds(start, size)],
+                from_core[k].at[pl.ds(j * size, size)],
+                core_send.at[k, j],
+                core_recv.at[k, j],
+                sibling,
+            )
+    pair_copies = [swap(shares[i], theirs[i], i) for i in range(pairs)]
     core_copies[last, 0].wait_recv()
     small_pair[...] = small[...] + small_core[...]
     side_copies[last, 0] = send(
         small_pair, small_side, side_send.at[last, 0], side_recv.at[last, 0], side
     )
-    for k in range(arrays):
+    for k, d in far_first:
         size = sums[k].shape[0]
-        for d in order:
-            j = length + d
-            core_copies[k, j].wait_recv()
-            mine = part_start(k, d, 1 - column, core)
-            add_into((from_core[k], j * size), [(from_core[k], j * size), (parts[k], mine)], size)
-            side_copies[k, d] = send(
-                from_core[k].at[pl.ds(j * size, size)],
-                from_side[k].at[pl.ds(d * size, size)],
-                side_send.at[k, d],
-                side_recv.at[k, d],
-                side,
-            )
+        j = length + d
+        core_copies[k, j].wait_recv()
+        mine = part_start(k, d, 1 - column, core)
+        add_into((from_core[k], j * size), [(from_core[k], j * size), (parts[k], mine)], size)
+        side_copies[k, d] = send(
+            from_core[k].at[pl.ds(j * size, size)],
+            from_side[k].at[pl.ds(d * size, size)],
+            side_send.at[k, d],
+            side_recv.at[k, d],
+            side,
+        )
     side_copies[last, 0].wait_recv()
     small_line[line] = small_pair[...] + small_side[...]
     for d in range(1, length):
@@ -367,32 +386,43 @@
             line_recv.at[last, d],
             ahead[d - 1],
         )
-    for k in range(arrays):
+    for k, d in far_first:
         size = sums[k].shape[0]
-        for d in order:
-            core_copies[k, d].wait_recv()
-            side_copies[k, d].wait_recv()
-            if d:
-                mine = part_start(k, d, column, core)
-                terms = [
-                    (from_side[k], d * size),
-                    (from_core[k], d * size),
-                    (parts[k], mine),
-                ]
-                add_into((from_side[k], d * size), terms, size)
-                line_copies[k, d] = send(
-                    from_side[k].at[pl.ds(d * size, size)],
-                    from_line[k].at[pl.ds((d - 1) * size, size)],
-                    line_send.at[k, d],
-                    line_recv.at[k, d],
-                    ahead[d - 1],
-                )
+        core_copies[k, d].wait_recv()
+        side_copies[k, d].wait_recv()
+        if d:
+            mine = part_start(k, d, column, core)
+            terms = [
+                (from_side[k], d * size),
+                (from_core[k], d * size),
+                (parts[k], mine),
+            ]
+            add_into((from_side[k], d * size), terms, size)
+            line_copies[k, d] = send(
+                from_side[k].at[pl.ds(d * size, size)],
+                from_line[k].at[pl.ds((d - 1) * size, size)],
+                line_send.at[k, d],
+                line_recv.at[k, d],
+                ahead[d - 1],
+            )
+    for i in range(pairs):
+        pair_copies[i].wait()
+
+        @pl.loop(0, shares[i].shape[0] // ADD_ROWS)
+        def _(step):
+            at = pl.ds(pl.multiple_of(step * ADD_ROWS, ADD_ROWS), ADD_ROWS)
+            totals[i][at, :] = shares[i][at, :].astype(jnp.float32) + theirs[i][at, :].astype(
+                jnp.float32
+            )
+
     for d in range(1, length):
         line_copies[last, d].wait_recv()
     total = small_line[0]
     for position in range(1, length):
         total = total + small_line[position]
     small_sum[...] = total
+    small_pairs = small_sum.at[:, pl.ds(0, paired_small)]
+    swap_small = swap(small_pairs, pair_small, pairs)
     for k in range(arrays):
         size = sums[k].shape[0]
         terms = [
@@ -404,22 +434,34 @@
             line_copies[k, d].wait_recv()
             terms.append((from_line[k], (d - 1) * size))
         add_into((sums[k], 0), terms, size)
+        if k == 0:
+            in_pairs = sums[0].at[:, pl.ds(paired[0], paired[1])]
+            swap_in = swap(in_pairs, pair_in, pairs + 1)
+    swap_small.wait()
+    small_pairs[...] = small_pairs[...] + pair_small[...]
+    swap_in.wait()
+    in_pairs[...] = in_pairs[...] + pair_in[...]
     for copies in (core_copies, side_copies, line_copies):
         for copy in copies.values():
             copy.wait_send()
 
 
-def scatter_rows(parts, small, count, collective_id):
+def scatter_rows(parts, small, shares, paired, paired_small, count, ways, collective_id):
     size = parts[0].shape[0] // count
-    if size % 16 or count % 4:
-        sums = tuple(
-            lax.psum_scatter(
-                part.astype(jnp.float32), "dp", scatter_dimension=0, tiled=True
-            )
+    if size % 16 or count % 4 or ways != 2:
+        sums = [
+            lax.psum_scatter(part.astype(jnp.float32), "dp", scatter_dimension=0, tiled=True)
             for part in parts
-        )
-        return sums + (lax.psum(small, "dp"),)
-    arrays, length = len(parts), count // 4
+        ]
+        left, right = paired[0], paired[0] + paired[1]
+        middle = lax.psum(sums[0][:, left:right], "tensor")
+        sums[0] = jnp.concatenate([sums[0][:, :left], middle, sums[0][:, right:]], axis=1)
+        small = lax.psum(small, "dp")
+        both = lax.psum(small[:, :paired_small], "tensor")
+        small = jnp.concatenate([both, small[:, paired_small:]], axis=1)
+        totals = [lax.psum(share, "tensor").astype(jnp.float32) for share in shares]
+        return (*sums, small, *totals)
+    arrays, pairs, length = len(parts), len(shares), count // 4
     vmem = pl.BlockSpec(memory_space=pltpu.VMEM)
     widths = [part.shape[1] for part in parts]
     received = [
@@ -428,12 +470,19 @@
         for width in widths
     ]
     return pl.pallas_call(
-        partial(scatter_kernel, count, arrays),
+        partial(scatter_kernel, count, arrays, pairs, paired, paired_small),
         out_shape=tuple(jax.ShapeDtypeStruct((size, width), jnp.float32) for width in widths)
-        + (jax.ShapeDtypeStruct(small.shape, jnp.float32),),
-        in_specs=[vmem] * (arrays + 1),
-        out_specs=(vmem,) * (arrays + 1),
-        scratch_shapes=received
+        + (jax.ShapeDtypeStruct(small.shape, jnp.float32),)
+        + tuple(jax.ShapeDtypeStruct(share.shape, jnp.float32) for share in shares),
+        in_specs=[vmem] * (arrays + 1 + pairs),
+        out_specs=(vmem,) * (arrays + 1 + pairs),
+        scratch_shapes=[pltpu.VMEM(share.shape, share.dtype) for share in shares]
+        + [
+            pltpu.VMEM((size, paired[1]), jnp.float32),
+            pltpu.VMEM((small.shape[0], paired_small), jnp.float32),
+        ]
+        + [pltpu.SemaphoreType.DMA((pairs + 2,))] * 2
+        + received
         + [pltpu.VMEM(small.shape, jnp.float32)] * 3
         + [pltpu.VMEM((length,) + small.shape, jnp.float32)]
         + [pltpu.SemaphoreType.DMA((arrays + 1, 2 * length))] * 2
@@ -441,7 +490,7 @@
         compiler_params=pltpu.CompilerParams(
             collective_id=collective_id, has_side_effects=True, vmem_limit_bytes=VMEM_BYTES
         ),
-    )(*parts, small)
+    )(*parts, small, *shares)
 
 
 def exchange_kernel(arrays, pieces, *refs):
@@ -540,7 +589,6 @@
         edges.append(edges[-1] + width)
     gain_in = packed_in[:, edges[7]]
     gain_mlp = packed_in[:, edges[7] + 1]
-    full_in = packed_in[:, : edges[7]]
     inputs = hidden_in.astype(jnp.float32)
     count_of_rows = inputs.shape[0]
     segment, token_position, live_rows = layout(seq_lengths, count_of_rows)
@@ -549,7 +597,7 @@
     visible = (segment[:, None] == segment[None, :]) & (row_index[None, :] <= row_index[:, None])
     normed_full, norm_in_pull = jax.vjp(root_norm, inputs, gain_in.astype(jnp.float32))
     normalized_input = normed_full.astype(jnp.bfloat16)
-    projected = product(normalized_input, full_in)
+    projected = product(normalized_input, packed_in)
     gate_ssm, conv_in, bc_raw, q_raw, k_raw, v_raw, step_raw = (
         projected[:, left:right] for left, right in zip(edges[:-1], edges[1:])
     )
@@ -592,8 +640,7 @@
     glu_pre = product(normed_mlp, full_glu)
     gate_pre, up_pre = glu_pre[:, :width_ff], glu_pre[:, width_ff:]
     activated = (jax.nn.silu(gate_pre) * up_pre).astype(jnp.bfloat16)
-    (mlp_out,) = tensor_sum((back_product(activated, down_t),), ways, 2)
-    layer_out = residual + live_column * mlp_out
+    mlp_share = back_product(activated, down_t).astype(jnp.bfloat16)
     grad_out = cotangent.astype(jnp.float32)
     grad_mlp = (live_column * grad_out).astype(jnp.bfloat16)
     grad_act = product(grad_mlp, down_t)
@@ -631,77 +678,69 @@
         grad_gated
     )
     bc_raw_share, conv_bc_share = bc_pull(bc_share)
-    grad_gate_ssm = grad_gate_ssm.astype(jnp.bfloat16)
-    grad_conv_in = grad_conv_in.astype(jnp.bfloat16)
-    grad_step = grad_step.astype(jnp.bfloat16)
     grad_projected = jnp.concatenate(
         [
-            grad_gate_ssm,
-            grad_conv_in,
+            grad_gate_ssm.astype(jnp.bfloat16),
+            grad_conv_in.astype(jnp.bfloat16),
             bc_raw_share.astype(jnp.bfloat16),
             grad_q,
             grad_k,
             grad_v,
-            grad_step,
+            grad_step.astype(jnp.bfloat16),
+            jnp.zeros((count_of_rows, packed_in.shape[1] - edges[7]), jnp.bfloat16),
         ],
         axis=1,
     )
+    norm_share = back_product(grad_projected, packed_in).astype(jnp.bfloat16)
+    _, gain_in_share = norm_in_pull(norm_share.astype(jnp.float32))
+    part_in = rows_product(normalized_input, grad_projected).astype(jnp.bfloat16)
     conv_rows = conv_bc.shape[0]
-    bc_terms = jnp.concatenate(
-        [bc_raw_share, jnp.pad(conv_bc_share, ((0, -conv_rows % 16), (0, 0)))], axis=0
-    )
-    grad_normed, bc_sums = tensor_sum(
-        (back_product(grad_projected, full_in), bc_terms), ways, 4
-    )
-    grad_bc_raw = bc_sums[:count_of_rows].astype(jnp.bfloat16)
-    part_conv_bc = bc_sums[count_of_rows : count_of_rows + conv_rows]
-    grad_input_norm, part_gain_in = norm_in_pull(grad_normed)
-    grad_in = grad_residual + grad_input_norm
-    grad_projected = jnp.concatenate(
-        [
-            grad_gate_ssm,
-            grad_conv_in,
-            grad_bc_raw,
-            grad_q,
-            grad_k,
-            grad_v,
-            grad_step,
-        ],
-        axis=1,
-    )
-    part_in = jnp.concatenate(
-        [
-            rows_product(normalized_input, grad_projected),
-            part_gain_in[:, None],
-            part_gain_mlp[:, None],
-        ],
-        axis=1,
-    ).astype(jnp.bfloat16)
-    part_in = jnp.pad(part_in, ((0, 0), (0, packed_in.shape[1] - part_in.shape[1])))
     head_rows, head_count = head_params.shape
+    model_width = inputs.shape[1]
     small = jnp.concatenate(
         [
+            jnp.pad(conv_bc_share, ((0, 8 - conv_rows), (0, 0))),
+            gain_in_share.reshape(8, model_width // 8),
+            part_gain_mlp.reshape(8, model_width // 8),
             jnp.pad(part_conv_x, ((0, 8 - conv_rows), (0, 0))),
-            jnp.pad(part_conv_bc, ((0, 8 - conv_rows), (0, 0))),
             jnp.pad(part_heads, ((0, 8 - head_rows), (0, -head_count % 128))),
         ],
         axis=1,
     )
-    sum_in, sum_out_o, sum_glu, sum_down, sum_small = scatter_rows(
-        (part_in, part_out, part_glu, part_down), small, count, 5
-    )
+    marks = [0]
+    for width in (width_bc, model_width // 8, model_width // 8, width_z, head_count):
+        marks.append(marks[-1] + width)
+    sum_in, sum_out_o, sum_glu, sum_down, sum_small, mlp_out, grad_normed = scatter_rows(
+        (part_in, part_out, part_glu, part_down),
+        small,
+        (mlp_share, norm_share),
+        (edges[2], width_bc),
+        marks[2],
+        count,
+        ways,
+        5,
+    )
+    layer_out = residual + live_column * mlp_out
+    grad_input_norm, _ = norm_in_pull(grad_normed)
+    grad_in = grad_residual + grad_input_norm
     sum_z, sum_x, sum_bc, sum_q, sum_k, sum_v, sum_dt = (
         sum_in[:, left:right] for left, right in zip(edges[:-1], edges[1:])
     )
-    sum_gain_in = sum_in[:, edges[7]]
-    sum_gain_mlp = sum_in[:, edges[7] + 1]
+    sum_conv_bc, all_gain_in, all_gain_mlp, sum_conv_x, sum_heads = (
+        sum_small[:, left:right] for left, right in zip(marks[:-1], marks[1:])
+    )
+    sum_conv_bc, sum_conv_x = sum_conv_bc[:conv_rows], sum_conv_x[:conv_rows]
+    sum_heads = sum_heads[:head_rows]
+    gain_size = norm_in.shape[0]
+    gain_start = lax.axis_index("dp") * gain_size
+    sum_gain_in, sum_gain_mlp = (
+        lax.dynamic_slice_in_dim(gain.reshape(model_width), gain_start, gain_size)
+        for gain in (all_gain_in, all_gain_mlp)
+    )
     sum_out = sum_out_o[:, :width_z].T
     sum_o = sum_out_o[:, width_z:].T
     sum_gate, sum_up = sum_glu[:, :width_ff], sum_glu[:, width_ff:]
     sum_down = sum_down.T
-    sum_conv_x = sum_small[:conv_rows, :width_z]
-    sum_conv_bc = sum_small[:conv_rows, width_z : width_z + width_bc]
-    sum_heads = sum_small[:head_rows, width_z + width_bc : width_z + width_bc + head_count]
     return (
         layer_out,
         grad_in,

time: 410 us -> 381 us (0.929)
  Pallas kernels: 244 us -> 216 us
  matrix products: 45.9 us -> 60.8 us
  local copies, waits for them, and re-layouts: 60.9 us -> 46.6 us
    pallas_call x4 -> x2, Pallas kernels: 56.6 us -> 28.6 us  [tensor_sum(): pl.pallas_call(partial(exchange_kernel, arrays, pieces), out_shape=tuple(...]
    unnamed x267 -> x197, local copies, waits for them, and re-layouts: 14.5 us -> 6.4 us
    dot_general x3, matrix products: 12 us -> 18.1 us  [state_mix(): result = jnp.einsum('hts,shp->thp', mixing, inputs, precision=EXACT_PRODUCT)]
    concatenate x3 -> x2, local copies, waits for them, and re-layouts: 8.57 us -> 2.51 us  [the longest x1 2.51 us: body(): jnp.concatenate([grad_gate_ssm.astype(jnp.bfloat16), grad_conv_in.astype(...]
    another operation x8 -> x6, local copies, waits for them, and re-layouts: 8.76 us -> 3.62 us
    pad x1 -> x0, local copies, waits for them, and re-layouts: 4.85 us -> none  [body(): jnp.pad(part_in, ((0, 0), (0, packed_in.shape[1] - part_in.shape[1])))]
where the time goes in v2:
time: 381 us; the launch traced here: 374 us
  Pallas kernels  216 us (57%)
  matrix products  60.8 us (16%)
  other arithmetic  47.5 us (12%)
  local copies, waits for them, and re-layouts  46.6 us (12%)
    pallas_call x1, Pallas kernels, scatter_rows(): pl.pallas_call(partial(scatter_kernel, count, arrays, pairs, paired, pair...  95.9 us
    pallas_call x1, Pallas kernels, gather_rows(): pl.pallas_call(partial(gather_kernel, count, arrays), out_shape=tuple((ja...  91.6 us
    pallas_call x2, Pallas kernels, tensor_sum(): pl.pallas_call(partial(exchange_kernel, arrays, pieces), out_shape=tuple(...  28.6 us
    dot_general x3, matrix products, state_mix(): result = jnp.einsum('hts,shp->thp', mixing, inputs, precision=EXACT_PRODUCT)  18.1 us
    dot_general x4, matrix products, back_product(): lax.dot_general(left_side, right_side, (((1,), (1,)), ((), ())), preferre...  11.7 us
    dot_general x4, matrix products, rows_product(): lax.dot_general(left_side, right_side, (((0,), (0,)), ((), ())), preferre...  11.5 us
    another operation x11, other arithmetic  9.24 us
    dot_general x4, matrix products, product(): return jnp.dot(left_side, right_side, preferred_element_type=jnp.float32)  7.83 us

profile of v2, /device:TPU:9, one launch (start us, length us, event | category | flops | bytes accessed | tf_op | source)
XLA Modules:
  0.0 373.5 jit_solution(17123079247516095902)
XLA Ops:
  1.6 1.8 concatenate.86.refs_0_
  3.3 1.7 pad_maximum_fusion.6.refs_2_
  5.0 1.6 pad_maximum_fusion.7.refs_1_
  6.6 91.6 %shard_map.339 = (bf16[1024,2304]{1,0:T(8,128)(2,1)}, bf16[1024,1024]{1,0:T(8,128)(2,1)}, bf16[1024,2048]{1,0:T(8,128)(2,1)}, bf16[1024,1024]{1,0:T(8,128)(2,1)}) custom-call(bf16[64,2304]{1,0:T(8,128)(2,1)} %concatenate.86.refs_0_, bf16[64,1024]{1,0:T(8,128)(2,1)} %pad_maximum_fusion.7.refs_1_, bf16[64,2048]{1,0:T(8,128)(2,1)} %pad_maximum_fusion.6.refs_2_, ...), custom_call_target="tpu_custom_call" | custom-call | tf_op jit(solution)/shard_map/pallas_call | solution.py:261
  98.2 1.5 convert_reduce_fusion
  99.9 3.8 %fusion.69 = f32[256,2304]{1,0:T(8,128)S(1)} fusion(bf16[1024,2304]{1,0:T(8,128)(2,1)} %get-tuple-element.30, bf16[256,1024]{1,0:T(8,128)(2,1)S(1)} %copy-done.4, f32[1024]{0:T(1024)S(1)} %get-tuple-element.137, f32[256]{0:T(256)S(1)} %fusion.106), kind=kOutput, calls=%fused_computation.136 | convolution fusion | flops 1209008128 | bytes 7607296 | tf_op jit(solution)/shard_map/dot_general | solution.py:20
  104.6 1.0 fusion.63
  105.6 1.1 fusion.79
  108.0 1.8 fusion.53
  109.8 1.4 copy.159
  113.7 5.8 %fusion.30 = f32[256,12,64]{0,2,1:T(8,128)} fusion(f32[256,12,64]{0,2,1:T(8,128)S(1)} %bitcast.178, f32[12,256]{1,0:T(8,128)S(1)} %copy.163, f32[12,256]{1,0:T(8,128)S(1)} %bitcast.196, f32[256,256]{1,0:T(8,128)} %fusion.79, pred[256,256]{1,0:T(8,128)(4,1)S(1)} %copy.160, f32[12]{0:T(128)} %get-tuple-element.214), kind=kOutput, calls=%fused_computation.43 | convolution fusion | flops 607518720 | bytes 1925168 | tf_op jit(solution)/shard_map/jvp(hts,shp->thp)/dot_general | solution.py:96
  119.5 1.4 copy.164
  122.0 1.1 copy.166
  125.0 1.2 fusion.130
  127.4 1.0 copy.169
  128.4 3.5 fusion.60.refs_0_
  131.9 14.9 %shard_map.340 = f32[256,1024]{1,0:T(8,128)S(1)} custom-call(f32[256,1024]{1,0:T(8,128)} %fusion.60.refs_0_), custom_call_target="tpu_custom_call" | custom-call | tf_op jit(solution)/shard_map/pallas_call | solution.py:536
  148.4 1.3 fusion.120
  150.2 2.0 multiply_convert_fusion.4
  152.2 2.3 fusion.54.refs_0_
  154.4 13.8 %shard_map.341 = f32[256,1024]{1,0:T(8,128)S(1)} custom-call(f32[256,1024]{1,0:T(8,128)} %fusion.54.refs_0_), custom_call_target="tpu_custom_call" | custom-call | tf_op jit(solution)/shard_map/pallas_call | solution.py:536
  171.2 1.7 multiply_reduce_fusion.6
  172.9 2.3 copy.171
  175.2 7.2 %fusion.7 = (f32[12,256]{1,0:T(8,128)S(1)}, f32[12,256]{1,0:T(8,128)S(1)}, f32[12,256]{1,0:T(8,128)}, f32[256,256]{1,0:T(8,128)}) fusion(f32[12,256]{1,0:T(8,128)} %copy-done.68, f32[12,256]{1,0:T(8,128)} %bitcast.197, f32[256,256]{1,0:T(8,128)} %fusion.79, pred[256,256]{1,0:T(8,128)(4,1)} %copy-done.43, f32[12,64,256]{2,1,0:T(8,128)} %bitcast.180, ...), kind=kOutput, calls=%fused_computation.18 | convolution fusion | flops 614128640 | bytes 2224128 | tf_op jit(solution)/shard_map/transpose(jvp(hts,shp->thp))/dot_general | solution.py:96
  183.0 1.3 add_any.101
  184.3 1.3 copy.181
  185.6 3.8 %reduce-window.21 = f32[12,2,128]{2,0,1:T(8,128)} reduce-window(f32[12,2,128]{2,0,1:T(8,128)} %copy.181, f32[]{:T(128)} %constant.26.clone.1), window={size=1x1x128 pad=0_0x0_0x0_127}, to_apply=%region_15.16 | reduce-window | flops 390144 | bytes 24580 | tf_op jit(solution)/shard_map/reduce-window.3
  189.4 1.4 slice_reduce_fusion
  190.8 1.3 reduce-window.24
  192.7 1.4 broadcast_add_fusion
  194.1 1.5 copy.182
  195.6 1.5 copy.180
  197.1 2.3 fusion.121
  199.3 1.2 bitcast_multiply_fusion.2
  202.0 1.3 pad_add_fusion.2
  203.3 5.2 %fusion.27 = f32[256,12,64]{0,2,1:T(8,128)} fusion(f32[12,64,256]{2,1,0:T(8,128)} %bitcast.181, f32[12,256]{1,0:T(8,128)} %copy-done.68, f32[12,256]{1,0:T(8,128)} %bitcast.198, f32[256,256]{1,0:T(8,128)} %fusion.79, pred[256,256]{1,0:T(8,128)(4,1)} %copy-done.43, f32[256,12,64]{0,2,1:T(8,128)} %bitcast.182, f32[12]{0:T(128)} %get-tuple-element.214), kind=kOutput, calls=%fused_computation.42 | convolution fusion | flops 607518720 | bytes 2711600 | tf_op jit(solution)/shard_map/transpose(jvp(hts,shp->thp))/dot_general | solution.py:96
  208.5 2.3 copy.172
  210.8 2.1 multiply_reduce_fusion.10
  213.0 1.0 multiply_reduce_fusion.9
  214.7 1.1 multiply_reduce_fusion.7
  216.5 1.6 slice.412
  218.1 1.7 copy.174
  219.7 2.3 fusion.37
  222.0 1.7 multiply_reduce_fusion.3
  225.9 1.5 copy.184
  227.4 1.3 convolution_bitcast_fusion.1
  230.2 1.7 copy.183
  231.8 1.6 fusion.81
  233.4 1.4 fusion.77
  234.8 1.8 multiply_reduce_fusion.14
  236.6 1.8 multiply_reduce_fusion.13
  240.4 2.0 multiply_reduce_fusion.11
  242.4 2.5 concatenate.106
  245.0 5.2 %fusion.39 = (f32[1024]{0:T(1024)S(1)}, bf16[256,1024]{1,0:T(8,128)(2,1)}) fusion(bf16[256,1024]{1,0:T(8,128)(2,1)} %param.20, f32[256]{0:T(256)} %copy-done.59, bf16[256,2304]{1,0:T(8,128)(2,1)S(1)} %concatenate.106, bf16[1024,2304]{1,0:T(8,128)(2,1)} %get-tuple-element.30), kind=kOutput, calls=%fused_computation.56 | convolution fusion | flops 1209531392 | bytes 6951936 | tf_op jit(solution)/shard_map/dot_general | solution.py:30
  250.4 3.4 convolution_convert_fusion.1.refs_2_
  253.8 2.2 convolution_convert_fusion.3.refs_1_
  256.1 3.7 convolution_convert_fusion.refs_0_
  260.8 2.2 convolution_convert_fusion.2.refs_3_
  263.0 95.9 %shard_map.342 = (f32[64,2304]{1,0:T(8,128)}, f32[64,1024]{1,0:T(8,128)S(1)}, f32[64,2048]{1,0:T(8,128)S(1)}, f32[64,1024]{1,0:T(8,128)S(1)}, f32[8,1408]{1,0:T(...) custom-call(bf16[1024,2304]{1,0:T(8,128)(2,1)} %convolution_convert_fusion.refs_0_, ...), custom_call_target="tpu_custom_call" | custom-call | tf_op jit(solution)/shard_map/pallas_call | solution.py:472
  358.9 1.7 fusion.126
  360.6 1.8 fusion.127
  362.5 1.5 fusion.43
  363.9 1.7 fusion.41
  366.5 1.5 fusion.125
  (280 shorter events, 31.4 us)
Async XLA Ops:
  0.7 99.0 %copy-start.4 = (bf16[256,1024]{1,0:T(8,128)(2,1)S(1)}, bf16[256,1024]{1,0:T(8,128)(2,1)}, u32[]{:S(2)}) copy-start(bf16[256,1024]{1,0:T(8,128)(2,1)} %param.20) | copy-start | bytes 1572868
  99.8 3.9 %copy-start.75 = (f32[256]{0:T(256)}, f32[256]{0:T(256)S(1)}, u32[]{:S(2)}) copy-start(f32[256]{0:T(256)S(1)} %fusion.42) | copy-start | bytes 3076
  99.9 3.9 %copy-start.59 = (f32[256]{0:T(256)}, f32[256]{0:T(256)S(1)}, u32[]{:S(2)}) copy-start(f32[256]{0:T(256)S(1)} %fusion.106) | copy-start | bytes 3076
  99.9 4.0 %copy-start.89 = (s32[4]{0:T(128)S(1)}, s32[4]{0:T(128)}, u32[]{:S(2)}) copy-start(s32[4]{0:T(128)} %param.21) | copy-start | bytes 52
  99.9 4.6 %copy-start.78 = (bf16[5,256]{1,0:T(8,128)(2,1)S(1)}, bf16[5,256]{1,0:T(8,128)(2,1)}, u32[]{:S(2)}) copy-start(bf16[5,256]{1,0:T(8,128)(2,1)} %param.28) | copy-start | bytes 7684
  104.2 2.9 copy-start.54
  104.2 2.9 copy-start.57
  104.2 2.9 copy-start.58
  104.5 2.3 copy-start.71
  104.6 2.3 copy-start.72
  104.6 2.3 copy-start.73
  104.6 2.3 copy-start.74
  105.6 4.2 %copy-start.26 = (f32[256,256]{1,0:T(8,128)}, f32[256,256]{1,0:T(8,128)S(1)}, u32[]{:S(2)}) copy-start(f32[256,256]{1,0:T(8,128)S(1)} %get-tuple-element.173) | copy-start | bytes 786436
  106.7 3.0 copy-start.11
  106.8 2.9 copy-start.13
  107.0 2.7 copy-start.46
  107.0 2.7 copy-start.48
  107.0 2.7 copy-start.50
  107.0 2.7 copy-start.52
  108.0 3.2 copy-start.88
  111.2 8.3 %copy-start.30 = (f32[256,768]{0,1:T(8,128)}, f32[256,768]{0,1:T(8,128)S(1)}, u32[]{:S(2)}) copy-start(f32[256,768]{0,1:T(8,128)S(1)} %copy.159) | copy-start | bytes 2359300
  113.3 7.6 %copy-start.69 = (f32[2,8,2,128]{3,1,2,0:T(8,128)}, f32[2,8,2,128]{3,1,2,0:T(8,128)S(1)}, u32[]{:S(2)}) copy-start(f32[2,8,2,128]{3,1,2,0:T(8,128)S(1)} %copy.197) | copy-start | bytes 49156
  113.4 7.5 %copy-start.68 = (f32[12,256]{1,0:T(8,128)}, f32[12,256]{1,0:T(8,128)S(1)}, u32[]{:S(2)}) copy-start(f32[12,256]{1,0:T(8,128)S(1)} %copy.163) | copy-start | bytes 36868
  113.7 7.2 %copy-start.43 = (pred[256,256]{1,0:T(8,128)(4,1)}, pred[256,256]{1,0:T(8,128)(4,1)S(1)}, u32[]{:S(2)}) copy-start(pred[256,256]{1,0:T(8,128)(4,1)S(1)} %copy.160) | copy-start | bytes 196612
  120.9 4.0 %copy-start.8 = (f32[256,768]{1,0:T(8,128)}, f32[256,768]{1,0:T(8,128)S(1)}, u32[]{:S(2)}) copy-start(f32[256,768]{1,0:T(8,128)S(1)} %copy.164) | copy-start | bytes 2359300
  123.1 4.2 %copy-start.61 = (f32[256]{0:T(256)}, f32[256]{0:T(256)S(1)}, u32[]{:S(2)}) copy-start(f32[256]{0:T(256)S(1)} %subtract_convert_fusion.2) | copy-start | bytes 3076
  123.1 4.2 %copy-start.79 = (f32[32]{0:T(128)}, f32[32]{0:T(128)S(1)}, u32[]{:S(2)}) copy-start(f32[32]{0:T(128)S(1)} %multiply_power_fusion) | copy-start | bytes 388
  124.6 2.7 copy-start.37
  126.2 5.8 %copy-start = (f32[1,4,256,256]{2,3,1,0:T(8,128)}, f32[1,4,256,256]{2,3,1,0:T(8,128)S(1)}, u32[]{:S(2)}) copy-start(f32[1,4,256,256]{2,3,1,0:T(8,128)S(1)} %get-tuple-element.224) | copy-start | bytes 3145732
  127.4 19.4 %copy-start.93 = (s32[4,1]{0,1:T(1,128)S(1)}, s32[4,1]{0,1:T(1,128)}, u32[]{:S(2)}) copy-start(s32[4,1]{0,1:T(1,128)} %copy-done.92) | copy-start | bytes 52
  128.4 19.6 %copy-start.5 = (bf16[256,1024]{1,0:T(8,128)(2,1)S(1)}, bf16[256,1024]{1,0:T(8,128)(2,1)}, u32[]{:S(2)}) copy-start(bf16[256,1024]{1,0:T(8,128)(2,1)} %param.20) | copy-start | bytes 1572868
  131.9 16.5 %copy-start.19 = (bf16[1024,2048]{1,0:T(8,128)(2,1)S(1)}, bf16[1024,2048]{1,0:T(8,128)(2,1)}, u32[]{:S(2)}) copy-start(bf16[1024,2048]{1,0:T(8,128)(2,1)} %get-tuple-element.33) | copy-start | bytes 12582916
  148.4 20.7 %copy-start.44 = (f32[256]{0:T(256)}, f32[256]{0:T(256)S(1)}, u32[]{:S(2)}) copy-start(f32[256]{0:T(256)S(1)} %fusion.107) | copy-start | bytes 3076
  152.2 2.3 copy-start.31
  152.2 2.3 copy-start.33
  208.5 4.5 %copy-start.55 = (f32[256]{0:T(256)S(1)}, f32[256]{0:T(256)}, u32[]{:S(2)}) copy-start(f32[256]{0:T(256)} %copy-done.54) | copy-start | bytes 3076
  210.8 3.2 copy-start.53
  214.2 2.2 copy-start.64
  214.2 2.2 copy-start.66
  219.7 4.0 %copy-start.1 = (f32[1,4,256,256]{2,3,1,0:T(8,128)S(1)}, f32[1,4,256,256]{2,3,1,0:T(8,128)}, u32[]{:S(2)}) copy-start(f32[1,4,256,256]{2,3,1,0:T(8,128)} %copy-done) | copy-start | bytes 3145732
  219.7 5.0 %copy-start.38 = (bf16[256,4,32]{0,2,1:T(8,128)(2,1)S(1)}, bf16[256,4,32]{0,2,1:T(8,128)(2,1)}, u32[]{:S(2)}) copy-start(bf16[256,4,32]{0,2,1:T(8,128)(2,1)} %copy-done.37) | copy-start | bytes 196612
  219.7 5.0 %copy-start.39 = (bf16[256,4,32]{0,2,1:T(8,128)(2,1)S(1)}, bf16[256,4,32]{0,2,1:T(8,128)(2,1)}, u32[]{:S(2)}) copy-start(bf16[256,4,32]{0,2,1:T(8,128)(2,1)} %get-tuple-element.199) | copy-start | bytes 196612
  222.0 3.0 copy-start.62
  222.0 3.0 copy-start.80
  224.8 11.8 %copy-start.56 = (f32[256]{0:T(256)S(1)}, f32[256]{0:T(256)}, u32[]{:S(2)}) copy-start(f32[256]{0:T(256)} %copy-done.54) | copy-start | bytes 3076
  244.9 5.3 %copy-start.16 = (bf16[256,2304]{1,0:T(8,128)(2,1)}, bf16[256,2304]{1,0:T(8,128)(2,1)S(1)}, u32[]{:S(2)}) copy-start(bf16[256,2304]{1,0:T(8,128)(2,1)S(1)} %concatenate.106) | copy-start | bytes 3538948
  244.9 5.3 %copy-start.83 = (f32[256]{0:T(256)S(1)}, f32[256]{0:T(256)}, u32[]{:S(2)}) copy-start(f32[256]{0:T(256)} %get-tuple-element.164) | copy-start | bytes 3076
  244.9 5.3 %copy-start.84 = (f32[256]{0:T(256)S(1)}, f32[256]{0:T(256)}, u32[]{:S(2)}) copy-start(f32[256]{0:T(256)} %get-tuple-element.167) | copy-start | bytes 3076
  244.9 5.3 %copy-start.85 = (f32[256]{0:T(256)S(1)}, f32[256]{0:T(256)}, u32[]{:S(2)}) copy-start(f32[256]{0:T(256)} %get-tuple-element.201) | copy-start | bytes 3076
  244.9 5.3 %copy-start.86 = (f32[256]{0:T(256)S(1)}, f32[256]{0:T(256)}, u32[]{:S(2)}) copy-start(f32[256]{0:T(256)} %get-tuple-element.146) | copy-start | bytes 3076
  244.9 5.3 %copy-start.87 = (f32[256]{0:T(256)S(1)}, f32[256]{0:T(256)}, u32[]{:S(2)}) copy-start(f32[256]{0:T(256)} %get-tuple-element.147) | copy-start | bytes 3076
  245.0 5.3 %copy-start.67 = (f32[1024]{0:T(1024)S(1)}, f32[1024]{0:T(1024)}, u32[]{:S(2)}) copy-start(f32[1024]{0:T(1024)} %get-tuple-element.142) | copy-start | bytes 12292
  245.0 5.3 %copy-start.40 = (f32[5,768]{1,0:T(8,128)S(1)}, f32[5,768]{1,0:T(8,128)}, u32[]{:S(2)}) copy-start(f32[5,768]{1,0:T(8,128)} %pad_add_fusion) | copy-start | bytes 46084
  245.0 5.4 %copy-start.77 = (f32[3,12]{1,0:T(4,128)S(1)}, f32[3,12]{1,0:T(4,128)}, u32[]{:S(2)}) copy-start(f32[3,12]{1,0:T(4,128)} %pad_add_fusion.2) | copy-start | bytes 436
  245.0 5.4 %copy-start.32 = (bf16[256,1024]{1,0:T(8,128)(2,1)S(1)}, bf16[256,1024]{1,0:T(8,128)(2,1)}, u32[]{:S(2)}) copy-start(bf16[256,1024]{1,0:T(8,128)(2,1)} %copy-done.31) | copy-start | bytes 1572868
  245.0 5.4 %copy-start.34 = (bf16[256,1024]{1,0:T(8,128)(2,1)S(1)}, bf16[256,1024]{1,0:T(8,128)(2,1)}, u32[]{:S(2)}) copy-start(bf16[256,1024]{1,0:T(8,128)(2,1)} %copy-done.33) | copy-start | bytes 1572868
  245.0 5.4 %copy-start.45 = (f32[256]{0:T(256)S(1)}, f32[256]{0:T(256)}, u32[]{:S(2)}) copy-start(f32[256]{0:T(256)} %copy-done.44) | copy-start | bytes 3076
  250.4 3.4 copy-start.3
  250.4 3.4 copy-start.22
  256.0 3.7 copy-start.35
  256.0 3.7 copy-start.91
  358.9 5.0 %copy-start.76 = (f32[256]{0:T(256)S(1)}, f32[256]{0:T(256)}, u32[]{:S(2)}) copy-start(f32[256]{0:T(256)} %copy-done.75) | copy-start | bytes 3076
  358.9 5.0 %copy-start.20 = (f32[256,1024]{1,0:T(8,128)S(1)}, f32[256,1024]{1,0:T(8,128)}, u32[]{:S(2)}) copy-start(f32[256,1024]{1,0:T(8,128)} %get-tuple-element.35) | copy-start | bytes 3145732
  358.9 5.0 %copy-start.29 = (f32[256,1024]{1,0:T(8,128)S(1)}, f32[256,1024]{1,0:T(8,128)}, u32[]{:S(2)}) copy-start(f32[256,1024]{1,0:T(8,128)} %get-tuple-element.34) | copy-start | bytes 3145732
  (30 other events, 42.9 us)
